TPU v7x, 128 devices: a whole 4x4x4 slice. The times are simulated.
128 devices in a mesh: ctx: 16 (over x, z), dp: 8 (over y, core).
Axes of the slice: x: 4, y: 4, z: 4, core: 2. Of those that a mesh axis runs over, the one named last changes fastest.
Arguments:
- queries: bfloat16 [8, 2048, 8192], P('dp', 'ctx'), may hold values from -25 to 25
- grad_out: bfloat16 [8, 2048, 8192], P('dp', 'ctx'), may hold values from -6 to 6
- key_raw: bfloat16 [8, 16, 256, 1024], P('dp', 'ctx'), may hold values from -5 to 5
- values: bfloat16 [8, 16, 256, 1024], P('dp', 'ctx'), may hold values from -6 to 6
- key_gain: float32 [128], replicated, may hold values from 0.5 to 1.5
- image_pos: int32 [8, 16], P('dp', 'ctx'), may hold values from 0 to 127, as said below
Outputs:
- grad_queries: bfloat16 [8, 2048, 8192], P('dp', 'ctx')
- grad_key_raw: bfloat16 [8, 16, 256, 1024], P('dp', 'ctx')
- grad_values: bfloat16 [8, 16, 256, 1024], P('dp', 'ctx')
- grad_gain: float32 [128], replicated
Inputs may be any that keep to these rules, and one draw needn't show every extreme that they name: `image_pos`: the image of the first shard of each row stands at position 0 and that of the last shard at 127.
All inputs are finite; a program needn't handle non-finite values.
Results may differ from a plain program's by a relative error of at most 0.0054.
The roundings to bfloat16 on the way count: a program that leaves them out, or rounds other values in their place, can miss the bound.
Values may be sent and summed in bfloat16 or wider, within the bound.
No kernel may reach another device: no remote copies, remote signals or barrier semaphores. Data moves between devices by JAX's collectives and lax.ppermute only.
A program may use at most 320 MiB of HBM per device.

v0:
```python
import jax
import jax.numpy as jnp
from jax import lax
from jax.sharding import PartitionSpec as P

DOC_IMG = 4


def shifted(value, axis, steps):
    count = lax.axis_size(axis)
    initial, last = (max(0, -steps), min(count, count - steps))
    return lax.ppermute(value, axis, [(source, source + steps) for source in range(initial, last)])


def shards(queries, grad_out, key_raw, values, key_gain, image_pos):
    head_dim = key_gain.shape[0]
    mem_rows = key_raw.shape[2]
    kv_heads = key_raw.shape[3] // head_dim
    tok_rows = queries.shape[1]
    group_size = queries.shape[2] // head_dim // kv_heads
    scaling = head_dim ** (-0.5)
    span_len = DOC_IMG + 1
    span_rows = span_len * mem_rows
    shaped = key_raw[0, 0].astype(jnp.float32).reshape(mem_rows, kv_heads, head_dim)
    inv_rms = lax.rsqrt(jnp.mean(shaped * shaped, -1, keepdims=True) + 1e-05)
    unit_keys = shaped * inv_rms
    own_keys = (unit_keys * key_gain).astype(jnp.bfloat16).reshape(mem_rows, kv_heads * head_dim)
    own_values = values[0, 0]
    shard_id = lax.axis_index("ctx")
    position = image_pos[0, 0]
    tok_index = jnp.arange(tok_rows, dtype=jnp.int32)
    last_image = jnp.where(tok_index >= position, shard_id, shard_id - 1)
    first_image = last_image // DOC_IMG * DOC_IMG
    blocks = [(own_keys, own_values)]
    for distance in range(1, span_len):
        blocks.append(shifted((own_keys, own_values), "ctx", distance))
    key_span = jnp.concatenate([block[0] for block in blocks], 0)
    value_span = jnp.concatenate([block[1] for block in blocks], 0)
    image_ids = shard_id - jnp.arange(span_rows, dtype=jnp.int32) // mem_rows
    visible = (first_image[:, None] <= image_ids[None, :]) & (
        image_ids[None, :] <= last_image[:, None]
    )
    query_heads = queries[0].reshape(tok_rows, kv_heads, group_size, head_dim)
    grad_heads = grad_out[0].reshape(tok_rows, kv_heads, group_size, head_dim)
    dq_list = []
    dk_list = []
    dv_list = []
    for head in range(kv_heads):
        query_part = query_heads[:, head]
        grad_part = grad_heads[:, head]
        key_part = key_span[:, head * head_dim : (head + 1) * head_dim]
        value_part = value_span[:, head * head_dim : (head + 1) * head_dim]
        scores = (
            jnp.einsum("tgd,rd->gtr", query_part, key_part, preferred_element_type=jnp.float32)
            * scaling
        )
        dprob = jnp.einsum("tgd,rd->gtr", grad_part, value_part, preferred_element_type=jnp.float32)
        masked = visible[None]
        row_max = jnp.max(jnp.where(masked, scores, -1e30), -1, keepdims=True)
        total = jnp.sum(jnp.where(masked, jnp.exp(scores - row_max), 0.0), -1, keepdims=True)
        log_total = row_max + jnp.log(total)
        prob = jnp.where(masked, jnp.exp(scores - log_total), 0.0)
        delta = jnp.sum(prob * dprob, -1, keepdims=True)
        prob_low = prob.astype(jnp.bfloat16)
        dscore = (prob * (dprob - delta)).astype(jnp.bfloat16)
        dq_list.append(
            scaling
            * jnp.einsum("gtr,rd->tgd", dscore, key_part, preferred_element_type=jnp.float32)
        )
        dk_list.append(
            scaling
            * jnp.einsum("gtr,tgd->rd", dscore, query_part, preferred_element_type=jnp.float32)
        )
        dv_list.append(
            jnp.einsum("gtr,tgd->rd", prob_low, grad_part, preferred_element_type=jnp.float32)
        )
    dq_total = jnp.stack(dq_list, 1)
    key_grads = jnp.concatenate(dk_list, -1)
    value_grads = jnp.concatenate(dv_list, -1)
    key_parts = [
        key_grads[distance * mem_rows : (distance + 1) * mem_rows] for distance in range(span_len)
    ]
    value_parts = [
        value_grads[distance * mem_rows : (distance + 1) * mem_rows] for distance in range(span_len)
    ]
    total_keys = key_parts[0]
    total_values = value_parts[0]
    for distance in range(1, span_len):
        received = shifted((key_parts[distance], value_parts[distance]), "ctx", -distance)
        total_keys = total_keys + received[0]
        total_values = total_values + received[1]
    grad_norm = total_keys.reshape(mem_rows, kv_heads, head_dim)
    partial_gain = jnp.sum(grad_norm * unit_keys, axis=(0, 1))
    grad_gain = lax.psum(partial_gain, ("ctx", "dp"))
    scaled = grad_norm * key_gain
    grad_key_raw = inv_rms * (scaled - unit_keys * jnp.mean(scaled * unit_keys, -1, keepdims=True))
    grad_key_raw = grad_key_raw.reshape(1, 1, mem_rows, kv_heads * head_dim).astype(jnp.bfloat16)
    grad_values = total_values.reshape(1, 1, mem_rows, kv_heads * head_dim).astype(jnp.bfloat16)
    grad_queries = dq_total.reshape(1, tok_rows, kv_heads * group_size * head_dim).astype(
        jnp.bfloat16
    )
    return (grad_queries, grad_key_raw, grad_values, grad_gain)


def solution(mesh):
    return jax.shard_map(
        shards,
        mesh=mesh,
        in_specs=(
            P("dp", "ctx", None),
            P("dp", "ctx", None),
            P("dp", "ctx", None, None),
            P("dp", "ctx", None, None),
            P(),
            P("dp", "ctx"),
        ),
        out_specs=(
            P("dp", "ctx", None),
            P("dp", "ctx", None, None),
            P("dp", "ctx", None, None),
            P(),
        ),
        check_vma=False,
    )
```

profile of v0, /device:TPU:0, one launch (start us, length us, event | category | flops | bytes accessed | tf_op | source)
XLA Modules:
  0.0 544.1 jit_solution(7007177945545293675)
XLA Ops:
  5.6 4.7 collective-permute-start
  10.3 5.5 %collective-permute-start.1 = (bf16[256,1024]{1,0:T(8,128)(2,1)}, bf16[256,1024]{1,0:T(8,128)(2,1)}, u32[]{:S(2)}, u32[]{:S(2)}) collective-permute-start(bf16[256,1024]{1,0:T(8,128)(2,1)} %get-tuple-element.43), channel_id=1, source_target_pairs={{0,16},{8,24},{16,32},{24,40},{32,48},{40,56},{48,64},{56,72},{64,... | collective-permute-start | bytes 1572872 | tf_op jit(solution)/shard_map/ppermute | solution.py:12
  15.8 3.8 collective-permute-start.2
  19.7 3.4 collective-permute-start.3
  23.1 3.7 collective-permute-start.4
  27.8 4.1 copy.144
  31.8 4.1 copy.146
  37.2 1.7 collective-permute-start.5
  40.0 10.6 %collective-permute-start.6 = (bf16[256,1024]{1,0:T(8,128)(2,1)}, bf16[256,1024]{1,0:T(8,128)(2,1)S(1)}, u32[]{:S(2)}, u32[]{:S(2)}) collective-permute-start(bf16[256,1024]{1,0:T(8,128)(2,1)} %bitcast.8), channel_id=1, source_target_pairs={{0,24},{8,32},{16,40},{24,48},{32,56},{40,64},{48,72},{56,80},{64,... | collective-permute-start | bytes 1572872 | tf_op jit(solution)/shard_map/ppermute | solution.py:12
  51.7 3.9 collective-permute-start.7
  57.8 1.5 copy-done.15
  59.3 2.0 convolution_multiply_fusion.1
  61.3 3.6 convolution_multiply_fusion.2
  64.9 3.1 convolution_multiply_fusion.3
  68.1 3.1 convolution_multiply_fusion.4
  72.3 3.2 convolution_multiply_fusion.5
  75.6 3.1 convolution_multiply_fusion.6
  78.7 3.1 fusion.228
  81.8 3.2 fusion.224
  85.0 3.2 fusion.225
  88.2 3.2 fusion.226
  91.4 3.1 fusion.227
  95.5 4.2 fusion.6
  99.6 16.8 %fusion = (f32[8,128]{1,0:T(8,128)S(1)}, f32[8,128]{1,0:T(8,128)S(1)}, f32[8,128]{1,0:T(8,128)S(1)}, f32[8,128]{1,0:T(8,128)S(1)}, f32[8,128]{1,0:T(8,128)S(1)},...) fusion(f32[1280,128,8]{1,0,2:T(8,128)} %copy-done.2, ...), kind=kOutput, calls=%fused_computation.2 | convolution fusion | flops 360439808 | bytes 47980544 | tf_op jit(solution)/shard_map/tgd,rd->gtr/dot_general | solution.py:57
  116.4 6.4 %fusion.2 = (bf16[8,128,1280]{1,2,0:T(8,128)(2,1)}, f32[8,128]{1,0:T(8,128)S(1)}) fusion(f32[1280,128,8]{1,0,2:T(8,128)} %get-tuple-element.64, f32[1280,128,8]{1,0,2:T(8,128)} %copy-done.2, f32[8,128]{1,0:T(8,128)S(1)} %get-tuple-element.16, f32[8,128]{1,0:T(8,128)S(1)} %log_add_fusion, pred[128,1280]{0,1:T(8,128)(4,1)S(1)} %compare_and_fusion, ...), kind=kLoop, calls=%fused_computation.4 | loop fusion | flops 10484736 | bytes 18530304 | tf_op jit(solution)/shard_map/convert_element_type | solution.py:65
  122.9 2.9 fusion.123
  125.7 17.7 %fusion.9 = (f32[8,128]{1,0:T(8,128)S(1)}, f32[8,128]{1,0:T(8,128)S(1)}, f32[8,128]{1,0:T(8,128)S(1)}, f32[8,128]{1,0:T(8,128)S(1)}, f32[8,128]{1,0:T(8,128)S(1)...) fusion(f32[1280,128,8]{1,0,2:T(8,128)S(1)} %convolution_multiply_fusion.1, ...), kind=kOutput, calls=%fused_computation.16 | convolution fusion | flops 365683712 | bytes 47996928 | tf_op jit(solution)/shard_map/tgd,rd->gtr/dot_general | solution.py:57
  143.5 20.0 %fusion.18 = (f32[8,128]{1,0:T(8,128)S(1)}, f32[8,128]{1,0:T(8,128)S(1)}, f32[8,128]{1,0:T(8,128)S(1)}, f32[8,128]{1,0:T(8,128)S(1)}, f32[8,128]{1,0:T(8,128)S(1)}, /*index=5*/f32[1280,128,8]{1,0,2:T(8,128)}) fusion(f32[1280,128,8]{1,0,2:T(8,128)} %convolution_multiply_fusion.2, f32[8,128]{1,0:T(8,128)S(1)} %log_add_fusion.2, ...), kind=kOutput, calls=%fused_computation.30 | convolution fusion | flops 361753600 | bytes 53223424 | tf_op jit(solution)/shard_map/tgd,rd->gtr/dot_general | solution.py:57
  163.5 19.6 %fusion.11 = (bf16[8,128,1280]{1,2,0:T(8,128)(2,1)S(1)}, bf16[8,128,1280]{1,2,0:T(8,128)(2,1)}, bf16[8,128,1280]{1,2,0:T(8,128)(2,1)}, bf16[8,128,1280]{1,2,0:T(8,128)(2,1)}) fusion(f32[1280,128,8]{1,0,2:T(8,128)} %get-tuple-element.65, f32[1280,128,8]{1,0,2:T(8,128)} %copy-done, f32[8,128]{1,0:T(8,128)S(1)} %get-tuple-element.26, ...), kind=kLoop, calls=%fused_computation.18 | loop fusion | flops 26214400 | bytes 52625408 | tf_op jit(solution)/shard_map/convert_element_type | solution.py:65
  183.2 2.7 fusion.183
  185.9 2.9 fusion.207
  188.9 4.6 fusion.129
  193.5 1.9 fusion.135
  195.4 1.9 fusion.141
  197.3 1.9 fusion.147
  199.2 1.9 fusion.153
  201.1 1.9 fusion.159
  203.0 1.9 fusion.165
  204.9 4.5 fusion.243
  210.7 1.3 collective-permute-start.13
  212.0 1.3 collective-permute-start.14
  213.3 1.3 collective-permute-start.15
  214.6 1.8 fusion.181
  216.4 1.8 fusion.179
  218.2 2.3 copy-done.24
  220.5 11.6 %fusion.20 = (bf16[8,128,1280]{1,2,0:T(8,128)(2,1)}, bf16[8,128,1280]{1,2,0:T(8,128)(2,1)}, bf16[8,128,1280]{1,2,0:T(8,128)(2,1)}) fusion(f32[1280,128,8]{1,0,2:T(8,128)} %get-tuple-element.66, f32[1280,128,8]{1,0,2:T(8,128)S(1)} %bitcast.677, f32[8,128]{1,0:T(8,128)S(1)} %get-tuple-element.33, f32[8,128]{1,0:T(8,128)S(1)} %log_add_fusion.2, ...), kind=kLoop, calls=%fused_computation.32 | loop fusion | flops 19660800 | bytes 39510016 | tf_op jit(solution)/shard_map/convert_element_type | solution.py:65
  232.1 3.6 fusion.177
  235.8 1.7 fusion.175
  237.5 1.7 fusion.173
  239.2 1.7 fusion.171
  241.0 1.7 fusion.169
  242.7 4.6 fusion.244
  247.3 1.5 collective-permute-start.10
  251.4 1.3 collective-permute-start.11
  252.7 5.2 collective-permute-done.13
  259.2 22.6 %collective-permute-done.14 = f32[256,1024]{0,1:T(8,128)} collective-permute-done((f32[256,1024]{0,1:T(8,128)}, f32[256,1024]{0,1:T(8,128)}, u32[]{:S(2)}, u32[]{:S(2)}) %collective-permute-start.14) | collective-permute-done | bytes 1048608 | tf_op jit(solution)/shard_map/ppermute | solution.py:12
  284.9 1.3 copy-done.27
  286.2 4.3 copy.218
  290.5 94.3 %collective-permute-done.15 = f32[256,1024]{0,1:T(8,128)} collective-permute-done((f32[256,1024]{0,1:T(8,128)}, f32[256,1024]{0,1:T(8,128)}, u32[]{:S(2)}, u32[]{:S(2)}) %collective-permute-start.15) | collective-permute-done | bytes 1048608 | tf_op jit(solution)/shard_map/ppermute | solution.py:12
  384.8 2.8 fusion.219
  388.6 41.2 %collective-permute-done.11 = f32[256,1024]{1,0:T(8,128)} collective-permute-done((f32[256,1024]{1,0:T(8,128)}, f32[256,1024]{1,0:T(8,128)}, u32[]{:S(2)}, u32[]{:S(2)}) %collective-permute-start.11) | collective-permute-done | bytes 1048608 | tf_op jit(solution)/shard_map/ppermute | solution.py:12
  429.8 3.4 multiply_reduce_fusion
  434.5 1.5 fusion.220
  436.0 108.0 %psum.7 = f32[128]{0:T(128)} all-reduce(f32[128]{0:T(128)S(1)} %bitcast_reduce_fusion), channel_id=1, replica_groups=mesh['ctx'=16,'dp'=8] {'ctx','dp'}, use_global_device_ids=true, to_apply=%region_28.29 | all-reduce | flops 128 | bytes 1024 | tf_op jit(solution)/shard_map/psum | solution.py:94
  (141 shorter events, 23.4 us)
Async XLA Ops:
  0.6 3.8 copy-start.23
  2.1 1.4 copy-start.19
  3.5 1.0 copy-start.11
  5.6 31.5 %collective-permute-start = (bf16[256,1024]{1,0:T(8,128)(2,1)}, bf16[256,1024]{1,0:T(8,128)(2,1)}, u32[]{:S(2)}, u32[]{:S(2)}) collective-permute-start(bf16[256,1024]{1,0:T(8,128)(2,1)} %get-tuple-element.43), channel_id=1, source_target_pairs={{0,8},{8,16},{16,24},{24,32},{32,40},{40,48},{48,56},{56,64},{64,7... | collective-permute-start | bytes 1572872 | tf_op jit(solution)/shard_map/ppermute | solution.py:12
  10.3 29.7 %collective-permute-start.1 = (bf16[256,1024]{1,0:T(8,128)(2,1)}, bf16[256,1024]{1,0:T(8,128)(2,1)}, u32[]{:S(2)}, u32[]{:S(2)}) collective-permute-start(bf16[256,1024]{1,0:T(8,128)(2,1)} %get-tuple-element.43), channel_id=1, source_target_pairs={{0,16},{8,24},{16,32},{24,40},{32,48},{40,56},{48,64},{56,72},{64,... | collective-permute-start | bytes 1572872 | tf_op jit(solution)/shard_map/ppermute | solution.py:12
  15.8 35.9 %collective-permute-start.2 = (bf16[256,1024]{1,0:T(8,128)(2,1)}, bf16[256,1024]{1,0:T(8,128)(2,1)}, u32[]{:S(2)}, u32[]{:S(2)}) collective-permute-start(bf16[256,1024]{1,0:T(8,128)(2,1)} %get-tuple-element.43), channel_id=1, source_target_pairs={{0,24},{8,32},{16,40},{24,48},{32,56},{40,64},{48,72},{56,80},{64,... | collective-permute-start | bytes 1572872 | tf_op jit(solution)/shard_map/ppermute | solution.py:12
  19.7 37.0 %collective-permute-start.3 = (bf16[256,1024]{1,0:T(8,128)(2,1)}, bf16[256,1024]{1,0:T(8,128)(2,1)}, u32[]{:S(2)}, u32[]{:S(2)}) collective-permute-start(bf16[256,1024]{1,0:T(8,128)(2,1)} %get-tuple-element.43), channel_id=1, source_target_pairs={{0,32},{8,40},{16,48},{24,56},{32,64},{40,72},{48,80},{56,88},{64,... | collective-permute-start | bytes 1572872 | tf_op jit(solution)/shard_map/ppermute | solution.py:12
  23.1 48.1 %collective-permute-start.4 = (bf16[256,1024]{1,0:T(8,128)(2,1)}, bf16[256,1024]{1,0:T(8,128)(2,1)}, u32[]{:S(2)}, u32[]{:S(2)}) collective-permute-start(bf16[256,1024]{1,0:T(8,128)(2,1)} %bitcast.8), channel_id=1, source_target_pairs={{0,8},{8,16},{16,24},{24,32},{32,40},{40,48},{48,56},{56,64},{64,7... | collective-permute-start | bytes 1572872 | tf_op jit(solution)/shard_map/ppermute | solution.py:12
  35.9 23.4 %copy-start.13 = (bf16[1,128,8192]{1,2,0:T(8,128)(2,1)S(1)}, bf16[1,128,8192]{1,2,0:T(8,128)(2,1)}, u32[]{:S(2)}) copy-start(bf16[1,128,8192]{1,2,0:T(8,128)(2,1)} %copy.144) | copy-start | bytes 6291460
  37.2 38.3 %collective-permute-start.5 = (bf16[256,1024]{1,0:T(8,128)(2,1)}, bf16[256,1024]{1,0:T(8,128)(2,1)S(1)}, u32[]{:S(2)}, u32[]{:S(2)}) collective-permute-start(bf16[256,1024]{1,0:T(8,128)(2,1)} %bitcast.8), channel_id=1, source_target_pairs={{0,16},{8,24},{16,32},{24,40},{32,48},{40,56},{48,64},{56,72},{64,... | collective-permute-start | bytes 1572872 | tf_op jit(solution)/shard_map/ppermute | solution.py:12
  40.0 35.5 %collective-permute-start.6 = (bf16[256,1024]{1,0:T(8,128)(2,1)}, bf16[256,1024]{1,0:T(8,128)(2,1)S(1)}, u32[]{:S(2)}, u32[]{:S(2)}) collective-permute-start(bf16[256,1024]{1,0:T(8,128)(2,1)} %bitcast.8), channel_id=1, source_target_pairs={{0,24},{8,32},{16,40},{24,48},{32,56},{40,64},{48,72},{56,80},{64,... | collective-permute-start | bytes 1572872 | tf_op jit(solution)/shard_map/ppermute | solution.py:12
  51.7 27.0 %collective-permute-start.7 = (bf16[256,1024]{1,0:T(8,128)(2,1)}, bf16[256,1024]{1,0:T(8,128)(2,1)S(1)}, u32[]{:S(2)}, u32[]{:S(2)}) collective-permute-start(bf16[256,1024]{1,0:T(8,128)(2,1)} %bitcast.8), channel_id=1, source_target_pairs={{0,32},{8,40},{16,48},{24,56},{32,64},{40,72},{48,80},{56,88},{64,... | collective-permute-start | bytes 1572872 | tf_op jit(solution)/shard_map/ppermute | solution.py:12
  57.8 1.5 copy-start.15
  59.3 2.0 copy-start.16
  61.3 64.4 %copy-start = (f32[1280,128,8]{1,0,2:T(8,128)}, f32[1280,128,8]{1,0,2:T(8,128)S(1)}, u32[]{:S(2)}) copy-start(f32[1280,128,8]{1,0,2:T(8,128)S(1)} %convolution_multiply_fusion.1) | copy-start | bytes 15728644
  75.5 3.2 copy-start.21
  78.7 12.7 %copy-start.25 = (bf16[1280,1024]{1,0:T(8,128)(2,1)}, bf16[1280,1024]{1,0:T(8,128)(2,1)S(1)}, u32[]{:S(2)}) copy-start(bf16[1280,1024]{1,0:T(8,128)(2,1)S(1)} %constant_dynamic-update-slice_fusion.5) | copy-start | bytes 7864324
  95.5 4.2 copy-start.2
  116.4 6.4 %copy-start.1 = (f32[1280,128,8]{1,0,2:T(8,128)S(1)}, f32[1280,128,8]{1,0,2:T(8,128)}, u32[]{:S(2)}) copy-start(f32[1280,128,8]{1,0,2:T(8,128)} %get-tuple-element.63) | copy-start | bytes 15728644
  183.1 2.8 copy-start.18
  183.2 5.7 %copy-start.22 = (bf16[1,128,8192]{1,2,0:T(8,128)(2,1)S(1)}, bf16[1,128,8192]{1,2,0:T(8,128)(2,1)}, u32[]{:S(2)}) copy-start(bf16[1,128,8192]{1,2,0:T(8,128)(2,1)} %copy.146) | copy-start | bytes 6291460
  183.2 10.3 %slice-start.2 = ((s8[5242880]{0:T(1024)(128)(4,1)}), s8[4194304]{0:T(1024)(128)(4,1)S(1)}, s32[]{:S(2)}) async-start(s8[5242880]{0:T(1024)(128)(4,1)} %bitcast.674), calls=%async_computation.2 | async-start | bytes 8388608
  185.9 7.5 %slice-start.3 = ((s8[5242880]{0:T(1024)(128)(4,1)}), s8[1048576]{0:T(1024)(128)(4,1)S(1)}, s32[]{:S(2)}) async-start(s8[5242880]{0:T(1024)(128)(4,1)} %bitcast.674), calls=%async_computation.3 | async-start | bytes 2097152
  185.9 9.4 %slice-start.8 = ((s8[5242880]{0:T(1024)(128)(4,1)}), s8[4194304]{0:T(1024)(128)(4,1)S(1)}, s32[]{:S(2)}) async-start(s8[5242880]{0:T(1024)(128)(4,1)} %bitcast.680), calls=%async_computation.8 | async-start | bytes 8388608
  188.9 6.5 %slice-start.9 = ((s8[5242880]{0:T(1024)(128)(4,1)}), s8[1048576]{0:T(1024)(128)(4,1)S(1)}, s32[]{:S(2)}) async-start(s8[5242880]{0:T(1024)(128)(4,1)} %bitcast.680), calls=%async_computation.9 | async-start | bytes 2097152
  188.9 8.4 %slice-start.6 = ((s8[5242880]{0:T(1024)(128)(4,1)}), s8[4194304]{0:T(1024)(128)(4,1)S(1)}, s32[]{:S(2)}) async-start(s8[5242880]{0:T(1024)(128)(4,1)} %bitcast.678), calls=%async_computation.6 | async-start | bytes 8388608
  193.5 3.8 slice-start.7
  193.5 5.7 %slice-start.4 = ((s8[5242880]{0:T(1024)(128)(4,1)}), s8[4194304]{0:T(1024)(128)(4,1)S(1)}, s32[]{:S(2)}) async-start(s8[5242880]{0:T(1024)(128)(4,1)} %bitcast.676), calls=%async_computation.4 | async-start | bytes 8388608
  195.4 3.9 slice-start.5
  195.4 5.8 %slice-start = ((s8[5242880]{0:T(1024)(128)(4,1)}), s8[4194304]{0:T(1024)(128)(4,1)S(1)}, s32[]{:S(2)}) async-start(s8[5242880]{0:T(1024)(128)(4,1)} %bitcast.672), calls=%async_computation | async-start | bytes 8388608
  197.3 3.9 slice-start.1
  197.3 5.7 %slice-start.10 = ((s8[5242880]{0:T(1024)(128)(4,1)}), s8[4194304]{0:T(1024)(128)(4,1)S(1)}, s32[]{:S(2)}) async-start(s8[5242880]{0:T(1024)(128)(4,1)} %bitcast.682), calls=%async_computation.10 | async-start | bytes 8388608
  199.2 3.8 slice-start.11
  204.9 9.7 %copy-start.5 = (bf16[8,128,1280]{1,2,0:T(8,128)(2,1)S(1)}, bf16[8,128,1280]{1,2,0:T(8,128)(2,1)}, u32[]{:S(2)}) copy-start(bf16[8,128,1280]{1,2,0:T(8,128)(2,1)} %get-tuple-element.56) | copy-start | bytes 7864324
  204.9 11.5 %copy-start.3 = (bf16[8,128,1280]{1,2,0:T(8,128)(2,1)S(1)}, bf16[8,128,1280]{1,2,0:T(8,128)(2,1)}, u32[]{:S(2)}) copy-start(bf16[8,128,1280]{1,2,0:T(8,128)(2,1)} %get-tuple-element.57) | copy-start | bytes 7864324
  209.4 42.0 %collective-permute-start.12 = (f32[256,1024]{0,1:T(8,128)}, f32[256,1024]{0,1:T(8,128)}, u32[]{:S(2)}, u32[]{:S(2)}) collective-permute-start(f32[256,1024]{0,1:T(8,128)} %get-tuple-element.44), channel_id=1, source_target_pairs={{8,0},{16,8},{24,16},{32,24},{40,32},{48,40},{56,48},{64,56},{72,6... | collective-permute-start | bytes 3145736 | tf_op jit(solution)/shard_map/ppermute | solution.py:12
  210.7 47.2 %collective-permute-start.13 = (f32[256,1024]{0,1:T(8,128)}, f32[256,1024]{0,1:T(8,128)}, u32[]{:S(2)}, u32[]{:S(2)}) collective-permute-start(f32[256,1024]{0,1:T(8,128)} %get-tuple-element.47), channel_id=1, source_target_pairs={{16,0},{24,8},{32,16},{40,24},{48,32},{56,40},{64,48},{72,56},{80,... | collective-permute-start | bytes 3145736 | tf_op jit(solution)/shard_map/ppermute | solution.py:12
  212.0 69.7 %collective-permute-start.14 = (f32[256,1024]{0,1:T(8,128)}, f32[256,1024]{0,1:T(8,128)}, u32[]{:S(2)}, u32[]{:S(2)}) collective-permute-start(f32[256,1024]{0,1:T(8,128)} %get-tuple-element.46), channel_id=1, source_target_pairs={{24,0},{32,8},{40,16},{48,24},{56,32},{64,40},{72,48},{80,56},{88,... | collective-permute-start | bytes 3145736 | tf_op jit(solution)/shard_map/ppermute | solution.py:12
  213.3 171.5 %collective-permute-start.15 = (f32[256,1024]{0,1:T(8,128)}, f32[256,1024]{0,1:T(8,128)}, u32[]{:S(2)}, u32[]{:S(2)}) collective-permute-start(f32[256,1024]{0,1:T(8,128)} %get-tuple-element.45), channel_id=1, source_target_pairs={{32,0},{40,8},{48,16},{56,24},{64,32},{72,40},{80,48},{88,56},{96,... | collective-permute-start | bytes 3145736 | tf_op jit(solution)/shard_map/ppermute | solution.py:12
  218.2 2.3 copy-start.24
  232.1 3.6 copy-start.8
  232.1 3.6 copy-start.14
  232.1 5.4 copy-start.7
  237.5 3.5 copy-start.10
  241.0 7.9 %copy-start.26 = (bf16[128,8,8,128]{0,3,2,1:T(8,128)(2,1)S(1)}, bf16[128,8,8,128]{0,3,2,1:T(8,128)(2,1)}, u32[]{:S(2)}) copy-start(bf16[128,8,8,128]{0,3,2,1:T(8,128)(2,1)} %fusion.207) | copy-start | bytes 6291460
  242.7 6.1 %copy-start.6 = (bf16[8,128,1280]{1,2,0:T(8,128)(2,1)S(1)}, bf16[8,128,1280]{1,2,0:T(8,128)(2,1)}, u32[]{:S(2)}) copy-start(bf16[8,128,1280]{1,2,0:T(8,128)(2,1)} %get-tuple-element.56) | copy-start | bytes 7864324
  242.7 6.2 %copy-start.17 = (bf16[1280,1024]{1,0:T(8,128)(2,1)S(1)}, bf16[1280,1024]{1,0:T(8,128)(2,1)}, u32[]{:S(2)}) copy-start(bf16[1280,1024]{1,0:T(8,128)(2,1)} %copy-done.15) | copy-start | bytes 7864324
  242.7 6.8 %copy-start.4 = (bf16[8,128,1280]{1,2,0:T(8,128)(2,1)S(1)}, bf16[8,128,1280]{1,2,0:T(8,128)(2,1)}, u32[]{:S(2)}) copy-start(bf16[8,128,1280]{1,2,0:T(8,128)(2,1)} %get-tuple-element.57) | copy-start | bytes 7864324
  247.3 2.8 copy-start.9
  247.3 141.3 %collective-permute-start.10 = (f32[256,1024]{1,0:T(8,128)}, f32[256,1024]{1,0:T(8,128)}, u32[]{:S(2)}, u32[]{:S(2)}) collective-permute-start(f32[256,1024]{1,0:T(8,128)} %get-tuple-element.50), channel_id=1, source_target_pairs={{24,0},{32,8},{40,16},{48,24},{56,32},{64,40},{72,48},{80,56},{88,... | collective-permute-start | bytes 3145736 | tf_op jit(solution)/shard_map/ppermute | solution.py:12
  251.4 178.3 %collective-permute-start.11 = (f32[256,1024]{1,0:T(8,128)}, f32[256,1024]{1,0:T(8,128)}, u32[]{:S(2)}, u32[]{:S(2)}) collective-permute-start(f32[256,1024]{1,0:T(8,128)} %get-tuple-element.49), channel_id=1, source_target_pairs={{32,0},{40,8},{48,16},{56,24},{64,32},{72,40},{80,48},{88,56},{96,... | collective-permute-start | bytes 3145736 | tf_op jit(solution)/shard_map/ppermute | solution.py:12
  257.9 171.9 %collective-permute-start.8 = (f32[256,1024]{1,0:T(8,128)}, f32[256,1024]{1,0:T(8,128)}, u32[]{:S(2)}, u32[]{:S(2)}) collective-permute-start(f32[256,1024]{1,0:T(8,128)} %get-tuple-element.48), channel_id=1, source_target_pairs={{8,0},{16,8},{24,16},{32,24},{40,32},{48,40},{56,48},{64,56},{72,6... | collective-permute-start | bytes 3145736 | tf_op jit(solution)/shard_map/ppermute | solution.py:12
  281.7 148.0 %collective-permute-start.9 = (f32[256,1024]{1,0:T(8,128)}, f32[256,1024]{1,0:T(8,128)}, u32[]{:S(2)}, u32[]{:S(2)}) collective-permute-start(f32[256,1024]{1,0:T(8,128)} %get-tuple-element.51), channel_id=1, source_target_pairs={{16,0},{24,8},{32,16},{40,24},{48,32},{56,40},{64,48},{72,56},{80,... | collective-permute-start | bytes 3145736 | tf_op jit(solution)/shard_map/ppermute | solution.py:12
  284.9 1.4 copy-start.27
  286.2 143.5 %copy-start.12 = (f32[256,8,128]{2,1,0:T(8,128)S(1)}, f32[256,8,128]{2,1,0:T(8,128)}, u32[]{:S(2)}) copy-start(f32[256,8,128]{2,1,0:T(8,128)} %copy-done.11) | copy-start | bytes 3145732
  388.6 44.8 %copy-start.28 = (f32[128]{0:T(128)S(1)}, f32[128]{0:T(128)}, u32[]{:S(2)}) copy-start(f32[128]{0:T(128)} %param.10) | copy-start | bytes 1540
  388.6 44.9 %copy-start.20 = (f32[32,8,8,128]{3,2,1,0:T(8,128)S(1)}, f32[32,8,8,128]{3,2,1,0:T(8,128)}, u32[]{:S(2)}) copy-start(f32[32,8,8,128]{3,2,1,0:T(8,128)} %copy-done.19) | copy-start | bytes 3145732
where the time goes:
time: 549 us; the launch traced here: 544 us
  waiting for transfers between devices  163 us (30%)
  matrix products  136 us (25%)
  blocking collectives  108 us (20%)
  other arithmetic  49.1 us (9%)
  starting transfers between devices  48 us (9%)
  local copies, waits for them, and re-layouts  37.3 us (7%)
    ppermute x16, waiting for transfers between devices, shifted(): lax.ppermute(value, axis, [(source, source + steps) for source in range(i...  163 us
    psum x1, blocking collectives, shards(): grad_gain = lax.psum(partial_gain, ('ctx', 'dp'))  108 us
    dot_general x8, matrix products, shards(): jnp.einsum('tgd,rd->gtr', grad_part, value_part, preferred_element_type=j...  70.3 us
    ppermute x16, starting transfers between devices, shifted(): lax.ppermute(value, axis, [(source, source + steps) for source in range(i...  48 us
    convert_element_type x3, other arithmetic, shards(): dscore = (prob * (dprob - delta)).astype(jnp.bfloat16)  37.6 us
    unnamed x95, local copies, waits for them, and re-layouts  25.8 us
    dot_general x8, matrix products, shards(): jnp.einsum('tgd,rd->gtr', query_part, key_part, preferred_element_type=jn...  23.2 us
    dot_general x8, matrix products, shards(): jnp.einsum('gtr,tgd->rd', prob_low, grad_part, preferred_element_type=jnp...  18.8 us
  transfers between devices with their start and end apart: 16, of which 4 were waited for; matrix products, arithmetic and copies ran while one was open for 14% of the time, Pallas kernels for 0%

commit v1 on v0

v1 whole, which is shorter than its diff:
```python
import functools

import jax
import jax.numpy as jnp
from jax import lax
import jax.experimental.pallas as pl
import jax.experimental.pallas.tpu as pltpu
from jax.sharding import PartitionSpec as P

DOC_IMG = 4
SPAN = DOC_IMG + 1
CHUNKS = 2
HD = 128
MASKED = -1e30
SCALE = HD**-0.5
LOG2E = 1.4426950408889634
NT = (((1,), (1,)), ((), ()))
TN = (((0,), (0,)), ((), ()))
NN = (((1,), (0,)), ((), ()))
VMEM_LIMIT = 40 * 2**20


def dot(left, right, dims):
    return lax.dot_general(left, right, dims, preferred_element_type=jnp.float32)


def unit_norm(raw):
    wide = raw.astype(jnp.float32)
    inv_rms = lax.rsqrt(jnp.mean(wide * wide, -1, keepdims=True) + 1e-05)
    return wide * inv_rms, inv_rms


def pack_kernel(key_ref, value_ref, out_ref):
    for head in range(key_ref.shape[1] // HD):
        left = 2 * HD * head
        out_ref[:, left : left + HD] = key_ref[:, HD * head : HD * (head + 1)]
        out_ref[:, left + HD : left + 2 * HD] = value_ref[:, HD * head : HD * (head + 1)]


def pack(key_raw, values, chunk):
    rows, width = key_raw.shape
    part = width // CHUNKS
    return pl.pallas_call(
        pack_kernel,
        grid=(1,),
        in_specs=[pl.BlockSpec((rows, part), lambda i: (0, chunk))] * 2,
        out_specs=pl.BlockSpec((rows, 2 * part), lambda i: (0, 0)),
        out_shape=jax.ShapeDtypeStruct((rows, 2 * part), key_raw.dtype),
        cost_estimate=pl.CostEstimate(flops=0, bytes_accessed=8 * rows * part, transcendentals=0),
    )(key_raw, values)


def head_work(
    images, meta, q_ref, do_ref, key_ref, value_ref, recv, gain_ref,
    dq_ref, own_k, own_v, parts, gain_part, s_ref, dp_ref, normed, dk_ref, dv_ref,
):
    shard, position = meta[0], meta[1]
    gain = gain_ref[...]
    tokens = q_ref.shape[0]
    group = q_ref.shape[1] // HD
    token = lax.broadcasted_iota(jnp.int32, (1, 2 * tokens), 1) % tokens
    bias = {}
    for i in images:
        raw = key_ref[...] if i == 0 else recv[i - 1][:, :HD]
        normed[i] = (unit_norm(raw)[0] * gain).astype(jnp.bfloat16)
        if i == 0:
            bias[i] = jnp.where(token >= position, 0.0, MASKED)
        elif len(images) == SPAN:
            bias[i] = jnp.where(token < position, 0.0, MASKED)
        else:
            bias[i] = jnp.where(i <= shard, 0.0, MASKED)
    for pair in range(group // 2):
        heads = [2 * pair, 2 * pair + 1]
        q_pair = jnp.concatenate([q_ref[:, g * HD : (g + 1) * HD] for g in heads], 0)
        do_pair = jnp.concatenate([do_ref[:, g * HD : (g + 1) * HD] for g in heads], 0)
        top = None
        for i in images:
            scores = dot(normed[i], q_pair, NT) * (SCALE * LOG2E) + bias[i]
            s_ref[i] = scores
            high = jnp.max(scores, 0, keepdims=True)
            top = high if top is None else jnp.maximum(top, high)
        total = 0.0
        weighted = 0.0
        for i in images:
            value = value_ref[...] if i == 0 else recv[i - 1][:, HD:]
            dprob = dot(value, do_pair, NT)
            weight = jnp.exp2(s_ref[i] - top)
            s_ref[i] = weight
            dp_ref[i] = dprob
            total = total + jnp.sum(weight, 0, keepdims=True)
            weighted = weighted + jnp.sum(weight * dprob, 0, keepdims=True)
        inverse = 1.0 / total
        delta = weighted * inverse
        dq_turned = 0.0
        for i in images:
            prob = s_ref[i] * inverse
            prob_low = prob.astype(jnp.bfloat16)
            dscore = (prob * (dp_ref[i] - delta)).astype(jnp.bfloat16)
            dv = dot(prob_low, do_pair, NN)
            dk = dot(dscore, q_pair, NN)
            if pair == 0:
                dv_ref[i] = dv
                dk_ref[i] = dk
            else:
                dv_ref[i] += dv
                dk_ref[i] += dk
            dq_turned = dq_turned + dot(normed[i], dscore, TN)
        dq = (dq_turned.T * SCALE).astype(jnp.bfloat16)
        for j, g in enumerate(heads):
            dq_ref[:, g * HD : (g + 1) * HD] = dq[j * tokens : (j + 1) * tokens]
    gain_sum = jnp.zeros_like(gain)
    for i in images:
        raw = key_ref[...] if i == 0 else recv[i - 1][:, :HD]
        dk = dk_ref[i] * SCALE
        gain_sum = gain_sum + jnp.sum(dk * unit_norm(raw)[0], 0, keepdims=True)
        if i == 0:
            own_k[...] = dk
            own_v[...] = dv_ref[i]
        else:
            parts[i - 1][:, :HD] = dk.astype(jnp.bfloat16)
            parts[i - 1][:, HD:] = dv_ref[i].astype(jnp.bfloat16)
    gain_part[...] += gain_sum


def attend_kernel(meta, q_ref, do_ref, key_ref, value_ref, *rest, aliased):
    recv, gain_ref, rest = rest[:DOC_IMG], rest[DOC_IMG], rest[DOC_IMG + 1 :]
    if aliased:
        rest = rest[1:]
    dq_ref, own_k, own_v, *rest = rest
    parts, gain_part, scratch = rest[:DOC_IMG], rest[DOC_IMG], rest[DOC_IMG + 1 :]

    @pl.when(pl.program_id(0) == 0)
    def _():
        gain_part[...] = jnp.zeros_like(gain_part)

    args = (
        meta, q_ref, do_ref, key_ref, value_ref, recv, gain_ref,
        dq_ref, own_k, own_v, parts, gain_part, *scratch,
    )

    @pl.when(meta[0] == 0)
    def _():
        head_work(tuple(range(SPAN)), *args)

    @pl.when(meta[0] != 0)
    def _():
        head_work(tuple(range(DOC_IMG)), *args)


def attend(meta, queries, grad_out, key_raw, values, recv, gain, dq, chunk):
    tokens, width = queries.shape
    rows = key_raw.shape[0]
    kv_heads = key_raw.shape[1] // HD
    group = width // HD // kv_heads
    heads = kv_heads // CHUNKS
    first = chunk * heads
    wide = pl.BlockSpec((tokens, group * HD), lambda h: (0, first + h))
    own = pl.BlockSpec((rows, HD), lambda h: (0, first + h))
    part = pl.BlockSpec((rows, 2 * HD), lambda h: (0, h))
    local = pl.BlockSpec((rows, HD), lambda h: (0, h))
    single = pl.BlockSpec((1, HD), lambda h: (0, 0))
    in_specs = [pl.BlockSpec(memory_space=pltpu.SMEM), wide, wide, own, own]
    in_specs += [part] * DOC_IMG + [single]
    args = [meta, queries, grad_out, key_raw, values, *recv, gain]
    aliases = {}
    if dq is not None:
        aliases = {len(args): 0}
        in_specs.append(pl.BlockSpec(memory_space=pl.ANY))
        args.append(dq)
    f32, bf16 = jnp.float32, jnp.bfloat16
    outs = pl.pallas_call(
        functools.partial(attend_kernel, aliased=dq is not None),
        grid=(heads,),
        in_specs=in_specs,
        out_specs=[wide, local, local] + [part] * DOC_IMG + [single],
        out_shape=[jax.ShapeDtypeStruct(queries.shape, bf16)]
        + [jax.ShapeDtypeStruct((rows, heads * HD), f32)] * 2
        + [jax.ShapeDtypeStruct((rows, 2 * heads * HD), bf16)] * DOC_IMG
        + [jax.ShapeDtypeStruct((1, HD), f32)],
        scratch_shapes=[
            pltpu.VMEM((SPAN, rows, 2 * tokens), f32),
            pltpu.VMEM((SPAN, rows, 2 * tokens), f32),
            pltpu.VMEM((SPAN, rows, HD), bf16),
            pltpu.VMEM((SPAN, rows, HD), f32),
            pltpu.VMEM((SPAN, rows, HD), f32),
        ],
        input_output_aliases=aliases,
        compiler_params=pltpu.CompilerParams(vmem_limit_bytes=VMEM_LIMIT),
        cost_estimate=pl.CostEstimate(
            flops=10 * heads * group * tokens * SPAN * rows * HD,
            bytes_accessed=heads * (6 * group * tokens * HD + 24 * SPAN * rows * HD),
            transcendentals=heads * group * tokens * SPAN * rows,
        ),
    )(*args)
    return outs[0], outs[1], outs[2], outs[3 : 3 + DOC_IMG], outs[3 + DOC_IMG]


def finish_kernel(key_ref, own_k, own_v, *rest, aliased):
    back, gain_ref, rest = rest[:DOC_IMG], rest[DOC_IMG], rest[DOC_IMG + 1 :]
    if aliased:
        rest = rest[2:]
    gk_ref, gv_ref = rest
    unit, inv_rms = unit_norm(key_ref[...])
    dk, dv = own_k[...], own_v[...]
    for ref in back:
        dk = dk + ref[:, :HD].astype(jnp.float32)
        dv = dv + ref[:, HD:].astype(jnp.float32)
    scaled = dk * gain_ref[...]
    inner = jnp.mean(scaled * unit, -1, keepdims=True)
    gk_ref[...] = (inv_rms * (scaled - unit * inner)).astype(gk_ref.dtype)
    gv_ref[...] = dv.astype(gv_ref.dtype)


def finish(key_raw, own_k, own_v, back, gain, done, chunk):
    rows, width = key_raw.shape
    heads = width // HD // CHUNKS
    first = chunk * heads
    local = pl.BlockSpec((rows, HD), lambda h: (0, h))
    part = pl.BlockSpec((rows, 2 * HD), lambda h: (0, h))
    placed = pl.BlockSpec((rows, HD), lambda h: (0, first + h))
    args = [key_raw, own_k, own_v, *back, gain]
    in_specs = [placed, local, local] + [part] * DOC_IMG + [pl.BlockSpec((1, HD), lambda h: (0, 0))]
    aliases = {}
    if done is not None:
        aliases = {len(args): 0, len(args) + 1: 1}
        in_specs += [pl.BlockSpec(memory_space=pl.ANY)] * 2
        args += done
    return pl.pallas_call(
        functools.partial(finish_kernel, aliased=done is not None),
        grid=(heads,),
        in_specs=in_specs,
        out_specs=[placed, placed],
        out_shape=[jax.ShapeDtypeStruct(key_raw.shape, jnp.bfloat16)] * 2,
        input_output_aliases=aliases,
        cost_estimate=pl.CostEstimate(
            flops=20 * rows * heads * HD, bytes_accessed=30 * rows * heads * HD, transcendentals=0
        ),
    )(*args)


def reader_pairs(count, distance):
    pairs = []
    for reader in range(distance, count):
        place = reader % DOC_IMG
        if place == 0 or distance <= place:
            pairs.append((reader - distance, reader))
    return pairs


def all_sum(value):
    for axis in ("dp", "ctx"):
        count = lax.axis_size(axis)
        step = 1
        while step < count:
            value = value + lax.ppermute(value, axis, [(i, i ^ step) for i in range(count)])
            step *= 2
    return value


def shards(queries, grad_out, key_raw, values, key_gain, image_pos):
    count = lax.axis_size("ctx")
    queries, grad_out = queries[0], grad_out[0]
    key_raw, values = key_raw[0, 0], values[0, 0]
    gain = key_gain[None]
    meta = jnp.stack([lax.axis_index("ctx") % DOC_IMG, image_pos[0, 0]]).astype(jnp.int32)
    pairs = [reader_pairs(count, distance) for distance in range(1, SPAN)]
    recv = []
    for chunk in range(CHUNKS):
        packed = pack(key_raw, values, chunk)
        recv.append([lax.ppermute(packed, "ctx", to) for to in pairs])
    dq = None
    gain_part = 0.0
    held = []
    for chunk in range(CHUNKS):
        dq, own_k, own_v, parts, part = attend(
            meta, queries, grad_out, key_raw, values, recv[chunk], gain, dq, chunk
        )
        gain_part = gain_part + part
        back = [
            lax.ppermute(value, "ctx", [(reader, owner) for owner, reader in to])
            for value, to in zip(parts, pairs)
        ]
        held.append((own_k, own_v, back))
    grad_gain = all_sum(gain_part)
    done = None
    for chunk, (own_k, own_v, back) in enumerate(held):
        done = finish(key_raw, own_k, own_v, back, gain, done, chunk)
    return dq[None], done[0][None, None], done[1][None, None], grad_gain[0]


def solution(mesh):
    return jax.shard_map(
        shards,
        mesh=mesh,
        in_specs=(
            P("dp", "ctx", None),
            P("dp", "ctx", None),
            P("dp", "ctx", None, None),
            P("dp", "ctx", None, None),
            P(),
            P("dp", "ctx"),
        ),
        out_specs=(
            P("dp", "ctx", None),
            P("dp", "ctx", None, None),
            P("dp", "ctx", None, None),
            P(),
        ),
        check_vma=False,
    )
```

time: 549 us -> 189 us (0.34)
  matrix products: 136 us -> 0 us
  blocking collectives: 108 us -> 0 us
  waiting for transfers between devices: 163 us -> 65.7 us
  Pallas kernels: 0 us -> 56.5 us
  other arithmetic: 49.1 us -> 0.61 us
  local copies, waits for them, and re-layouts: 37.3 us -> 6.42 us
  starting transfers between devices: 48 us -> 57 us
    dot_general x40 -> x0, matrix products: 136 us -> none  [the longest x8 70.3 us: shards(): jnp.einsum('tgd,rd->gtr', grad_part, value_part, preferred_element_type=j...]
    psum x1 -> x0, blocking collectives: 108 us -> none  [shards(): grad_gain = lax.psum(partial_gain, ('ctx', 'dp'))]
    ppermute x16 -> x23, waiting for transfers between devices: 163 us -> 65.7 us  [the longest x8 42.6 us: shards(): lax.ppermute(value, 'ctx', [(reader, owner) for owner, reader in to])]
    pallas_call x0 -> x6, Pallas kernels: none -> 56.5 us  [the longest x2 44.1 us: attend(): pl.pallas_call(functools.partial(attend_kernel, aliased=dq is not None),...]
    convert_element_type x5 -> x0, other arithmetic: 41.9 us -> none  [the longest x3 37.6 us: shards(): dscore = (prob * (dprob - delta)).astype(jnp.bfloat16)]
    unnamed x95 -> x34, local copies, waits for them, and re-layouts: 25.8 us -> 6.42 us
    slice x2 -> x0, local copies, waits for them, and re-layouts: 9.04 us -> none  [the longest x1 4.57 us: shards(): key_grads[distance * mem_rows:(distance + 1) * mem_rows]]
    ppermute x16 -> x23, starting transfers between devices: 48 us -> 57 us  [the longest x8 27.3 us: shards(): recv.append([lax.ppermute(packed, 'ctx', to) for to in pairs])]
  transfers between devices with their start and end apart: 16 -> 23, of which waited for: 4 -> 11; matrix products, arithmetic and copies ran while one was open for 14% -> 0% of each run, Pallas kernels for 0% -> 27%
where the time goes in v1:
time: 189 us; the launch traced here: 188 us
  waiting for transfers between devices  65.7 us (35%)
  starting transfers between devices  57 us (30%)
  Pallas kernels  56.5 us (30%)
  local copies, waits for them, and re-layouts  6.42 us (3%)
    pallas_call x2, Pallas kernels, attend(): pl.pallas_call(functools.partial(attend_kernel, aliased=dq is not None),...  44.1 us
    ppermute x8, waiting for transfers between devices, shards(): lax.ppermute(value, 'ctx', [(reader, owner) for owner, reader in to])  42.6 us
    ppermute x8, starting transfers between devices, shards(): recv.append([lax.ppermute(packed, 'ctx', to) for to in pairs])  27.3 us
    ppermute x7, starting transfers between devices, all_sum(): lax.ppermute(value, axis, [(i, i ^ step) for i in range(count)])  19.2 us
    ppermute x7, waiting for transfers between devices, all_sum(): lax.ppermute(value, axis, [(i, i ^ step) for i in range(count)])  13.3 us
    ppermute x8, starting transfers between devices, shards(): lax.ppermute(value, 'ctx', [(reader, owner) for owner, reader in to])  10.5 us
    ppermute x8, waiting for transfers between devices, shards(): recv.append([lax.ppermute(packed, 'ctx', to) for to in pairs])  9.75 us
    pallas_call x2, Pallas kernels, finish(): pl.pallas_call(functools.partial(finish_kernel, aliased=done is not None)...  8.25 us
  transfers between devices with their start and end apart: 23, of which 11 were waited for; matrix products, arithmetic and copies ran while one was open for 0% of the time, Pallas kernels for 27%

profile of v1, /device:TPU:0, one launch (start us, length us, event | category | flops | bytes accessed | tf_op | source)
XLA Modules:
  0.0 187.8 jit_solution(4909894023973997269)
XLA Ops:
  0.6 0.0 copy-start.1
  0.6 0.0 copy-start
  0.7 0.0 copy-start.6
  0.7 2.1 %shard_map.94 = bf16[256,1024]{1,0:T(8,128)(2,1)} custom-call(bf16[256,1024]{1,0:T(8,128)(2,1)} %bitcast.13, bf16[256,1024]{1,0:T(8,128)(2,1)} %bitcast.19), custom_call_target="tpu_custom_call" | custom-call | bytes 1048576 | tf_op jit(solution)/shard_map/pallas_call | solution.py:43
  2.8 4.3 %collective-permute-start.7 = (bf16[256,1024]{1,0:T(8,128)(2,1)}, bf16[256,1024]{1,0:T(8,128)(2,1)}, u32[]{:S(2)}, u32[]{:S(2)}) collective-permute-start(bf16[256,1024]{1,0:T(8,128)(2,1)} %shard_map.94), channel_id=1, source_target_pairs={{0,32},{32,64},{64,96},{1,33},{33,65},{65,97},{2,34},{34,66},{66,9... | collective-permute-start | bytes 1572872 | tf_op jit(solution)/shard_map/ppermute | solution.py:270
  7.1 4.0 %collective-permute-start.6 = (bf16[256,1024]{1,0:T(8,128)(2,1)}, bf16[256,1024]{1,0:T(8,128)(2,1)}, u32[]{:S(2)}, u32[]{:S(2)}) collective-permute-start(bf16[256,1024]{1,0:T(8,128)(2,1)} %shard_map.94), channel_id=1, source_target_pairs={{0,24},{8,32},{32,56},{40,64},{64,88},{72,96},{96,120},{1,25},{9,3... | collective-permute-start | bytes 1572872 | tf_op jit(solution)/shard_map/ppermute | solution.py:270
  11.1 2.1 %collective-permute-start.5 = (bf16[256,1024]{1,0:T(8,128)(2,1)}, bf16[256,1024]{1,0:T(8,128)(2,1)}, u32[]{:S(2)}, u32[]{:S(2)}) collective-permute-start(bf16[256,1024]{1,0:T(8,128)(2,1)} %shard_map.94), channel_id=1, source_target_pairs={{0,16},{8,24},{16,32},{32,48},{40,56},{48,64},{64,80},{72,88},{80,... | collective-permute-start | bytes 1572872 | tf_op jit(solution)/shard_map/ppermute | solution.py:270
  13.2 3.5 %collective-permute-start.4 = (bf16[256,1024]{1,0:T(8,128)(2,1)}, bf16[256,1024]{1,0:T(8,128)(2,1)}, u32[]{:S(2)}, u32[]{:S(2)}) collective-permute-start(bf16[256,1024]{1,0:T(8,128)(2,1)} %shard_map.94), channel_id=1, source_target_pairs={{0,8},{8,16},{16,24},{24,32},{32,40},{40,48},{48,56},{56,64},{64,7... | collective-permute-start | bytes 1572872 | tf_op jit(solution)/shard_map/ppermute | solution.py:270
  16.7 2.0 %shard_map.93 = bf16[256,1024]{1,0:T(8,128)(2,1)} custom-call(bf16[256,1024]{1,0:T(8,128)(2,1)} %bitcast.14, bf16[256,1024]{1,0:T(8,128)(2,1)} %bitcast.20), custom_call_target="tpu_custom_call" | custom-call | bytes 1048576 | tf_op jit(solution)/shard_map/pallas_call | solution.py:43
  18.7 3.1 %collective-permute-start.3 = (bf16[256,1024]{1,0:T(8,128)(2,1)}, bf16[256,1024]{1,0:T(8,128)(2,1)}, u32[]{:S(2)}, u32[]{:S(2)}) collective-permute-start(bf16[256,1024]{1,0:T(8,128)(2,1)} %shard_map.93), channel_id=1, source_target_pairs={{0,32},{32,64},{64,96},{1,33},{33,65},{65,97},{2,34},{34,66},{66,9... | collective-permute-start | bytes 1572872 | tf_op jit(solution)/shard_map/ppermute | solution.py:270
  22.5 0.1 pad_add_fusion.meta
  22.5 0.0 collective-permute-done.7.rest_3_
  22.6 1.9 collective-permute-start.2
  24.4 9.7 %collective-permute-done.6.rest_2_ = bf16[256,1024]{1,0:T(8,128)(2,1)} collective-permute-done((bf16[256,1024]{1,0:T(8,128)(2,1)}, bf16[256,1024]{1,0:T(8,128)(2,1)}, u32[]{:S(2)}, u32[]{:S(2)}) %collective-permute-start.6) | collective-permute-done | bytes 524320 | tf_op jit(solution)/shard_map/ppermute | solution.py:270
  34.1 1.3 collective-permute-start.1
  35.5 0.0 collective-permute-done.5.rest_1_
  35.5 7.1 %collective-permute-start = (bf16[256,1024]{1,0:T(8,128)(2,1)}, bf16[256,1024]{1,0:T(8,128)(2,1)S(1)}, u32[]{:S(2)}, u32[]{:S(2)}) collective-permute-start(bf16[256,1024]{1,0:T(8,128)(2,1)} %shard_map.93), channel_id=1, source_target_pairs={{0,8},{8,16},{16,24},{24,32},{32,40},{40,48},{48,56},{56,64},{64,7... | collective-permute-start | bytes 1572872 | tf_op jit(solution)/shard_map/ppermute | solution.py:270
  42.6 0.0 collective-permute-done.4.rest_0_
  42.6 0.0 copy-start.8
  42.6 1.6 copy-done.8
  44.2 22.0 %shard_map.95 = (bf16[128,8192]{1,0:T(8,128)(2,1)}, f32[256,512]{1,0:T(8,128)S(1)}, f32[256,512]{1,0:T(8,128)S(1)}, bf16[256,1024]{1,0:T(8,128)(2,1)S(1)}, bf16[...) custom-call(s32[2]{0:T(128)S(1)} %pad_add_fusion.meta, ...), custom_call_target="tpu_custom_call" | custom-call | flops 6710886400 | bytes 18874368 | tf_op jit(solution)/shard_map/pallas_call | solution.py:171
  66.3 0.8 copy-done.4
  67.1 0.8 copy-done.5
  67.9 1.3 collective-permute-start.12
  69.2 0.0 collective-permute-done.3.rest_3_
  69.2 1.3 collective-permute-start.13
  70.5 0.0 collective-permute-done.2.rest_2_
  70.5 1.5 collective-permute-start.14
  72.0 0.0 collective-permute-done.1.rest_1_
  72.0 0.0 collective-permute-done.rest_0_
  72.0 22.1 %shard_map.96 = (bf16[128,8192]{1,0:T(8,128)(2,1)}, f32[256,512]{1,0:T(8,128)S(1)}, f32[256,512]{1,0:T(8,128)S(1)}, bf16[256,1024]{1,0:T(8,128)(2,1)}, bf16[256,...) custom-call(s32[2]{0:T(128)S(1)} %pad_add_fusion.meta, ...), custom_call_target="tpu_custom_call", output_to_operand_aliasing={{0}: (10, {})} | custom-call | flops 6710886400 | bytes 18874368 | tf_op jit(solution)/shard_map/pallas_call | solution.py:171
  94.1 0.8 copy-done.2
  94.9 0.8 copy-done.3
  95.7 0.0 collective-permute-start.16
  95.7 1.1 collective-permute-done.16
  96.8 1.6 collective-permute-start.17
  98.4 2.0 %collective-permute-done.17 = f32[1,128]{1,0:T(1,128)S(1)} collective-permute-done((f32[1,128]{1,0:T(1,128)S(1)}, f32[1,128]{1,0:T(1,128)S(1)}, u32[]{:S(2)}, u32[]{:S(2)}) %collective-permute-start.17) | collective-permute-done | bytes 544 | tf_op jit(solution)/shard_map/ppermute | solution.py:255
  100.4 3.2 %collective-permute-start.18 = (f32[1,128]{1,0:T(1,128)S(1)}, f32[1,128]{1,0:T(1,128)S(1)}, u32[]{:S(2)}, u32[]{:S(2)}) collective-permute-start(f32[1,128]{1,0:T(1,128)S(1)} %add.31), channel_id=1, source_target_pairs={{0,4},{1,5},{2,6},{3,7},{4,0},{5,1},{6,2},{7,3},{8,12},{9,13},{10,... | collective-permute-start | bytes 1544 | tf_op jit(solution)/shard_map/ppermute | solution.py:255
  103.6 1.9 collective-permute-done.18
  105.4 0.0 collective-permute-start.19
  105.4 3.5 %collective-permute-done.19 = f32[1,128]{1,0:T(1,128)S(1)} collective-permute-done((f32[1,128]{1,0:T(1,128)S(1)}, f32[1,128]{1,0:T(1,128)S(1)}, u32[]{:S(2)}, u32[]{:S(2)}) %collective-permute-start.19) | collective-permute-done | bytes 544 | tf_op jit(solution)/shard_map/ppermute | solution.py:255
  109.0 1.9 %collective-permute-start.20 = (f32[1,128]{1,0:T(1,128)S(1)}, f32[1,128]{1,0:T(1,128)S(1)}, u32[]{:S(2)}, u32[]{:S(2)}) collective-permute-start(f32[1,128]{1,0:T(1,128)S(1)} %add.33), channel_id=1, source_target_pairs={{0,16},{8,24},{16,0},{24,8},{32,48},{40,56},{48,32},{56,40},{64,80... | collective-permute-start | bytes 1544 | tf_op jit(solution)/shard_map/ppermute | solution.py:255
  110.9 3.1 %collective-permute-done.20 = f32[1,128]{1,0:T(1,128)S(1)} collective-permute-done((f32[1,128]{1,0:T(1,128)S(1)}, f32[1,128]{1,0:T(1,128)S(1)}, u32[]{:S(2)}, u32[]{:S(2)}) %collective-permute-start.20) | collective-permute-done | bytes 544 | tf_op jit(solution)/shard_map/ppermute | solution.py:255
  114.0 7.6 %collective-permute-start.21 = (f32[1,128]{1,0:T(1,128)S(1)}, f32[1,128]{1,0:T(1,128)S(1)}, u32[]{:S(2)}, u32[]{:S(2)}) collective-permute-start(f32[1,128]{1,0:T(1,128)S(1)} %add.34), channel_id=1, source_target_pairs={{0,32},{8,40},{16,48},{24,56},{32,0},{40,8},{48,16},{56,24},{64,96... | collective-permute-start | bytes 1544 | tf_op jit(solution)/shard_map/ppermute | solution.py:255
  121.6 1.5 collective-permute-done.21
  123.1 4.9 %collective-permute-start.22 = (f32[1,128]{1,0:T(1,128)S(1)}, f32[1,128]{1,0:T(1,128)S(1)}, u32[]{:S(2)}, u32[]{:S(2)}) collective-permute-start(f32[1,128]{1,0:T(1,128)S(1)} %add.35), channel_id=1, source_target_pairs={{0,64},{8,72},{16,80},{24,88},{32,96},{40,104},{48,112},{56,120},{... | collective-permute-start | bytes 1544 | tf_op jit(solution)/shard_map/ppermute | solution.py:255
  128.0 1.3 collective-permute-start.15
  129.3 0.2 collective-permute-done.22
  129.5 1.3 collective-permute-start.8
  130.8 0.0 collective-permute-done.12.rest_0_
  130.8 1.3 collective-permute-start.9
  132.1 0.0 collective-permute-done.13.rest_1_
  132.2 1.3 collective-permute-start.10
  133.5 0.0 collective-permute-done.14.rest_2_
  133.5 1.3 collective-permute-start.11
  134.8 0.5 add_bitcast_fusion
  135.3 9.5 %collective-permute-done.15.rest_3_ = bf16[256,1024]{1,0:T(8,128)(2,1)S(1)} collective-permute-done((bf16[256,1024]{1,0:T(8,128)(2,1)S(1)}, bf16[256,1024]{1,0:T(8,128)(2,1)S(1)}, u32[]{:S(2)}, u32[]{:S(2)}) %collective-permute-start.15) | collective-permute-done | bytes 524320 | tf_op jit(solution)/shard_map/ppermute | solution.py:280
  144.8 0.8 copy-done.16
  145.6 4.1 %shard_map.97 = (bf16[256,1024]{1,0:T(8,128)(2,1)}, bf16[256,1024]{1,0:T(8,128)(2,1)}) custom-call(bf16[256,1024]{1,0:T(8,128)(2,1)} %bitcast.15, f32[256,512]{1,0:T(8,128)} %copy-done.4, f32[256,512]{1,0:T(8,128)} %copy-done.5, bf16[256,1024]{1,0:T(8,128)(2,1)} %copy-done.13, bf16[256,1024]{1,0:T(8,128)(2,1)} %copy-done.14, bf16[256,1024]{1,0:T(8,128)(2,1)} %copy-done.15, ...), custom_call_target="tpu_custom_call" | custom-call | flops 2621440 | bytes 3932160 | tf_op jit(solution)/shard_map/pallas_call | solution.py:228
  149.7 0.0 collective-permute-done.8.rest_0_
  149.7 3.7 %collective-permute-done.10.rest_2_ = bf16[256,1024]{1,0:T(8,128)(2,1)S(1)} collective-permute-done((bf16[256,1024]{1,0:T(8,128)(2,1)}, bf16[256,1024]{1,0:T(8,128)(2,1)S(1)}, u32[]{:S(2)}, u32[]{:S(2)}) %collective-permute-start.10) | collective-permute-done | bytes 524320 | tf_op jit(solution)/shard_map/ppermute | solution.py:280
  153.5 29.4 %collective-permute-done.11.rest_3_ = bf16[256,1024]{1,0:T(8,128)(2,1)S(1)} collective-permute-done((bf16[256,1024]{1,0:T(8,128)(2,1)}, bf16[256,1024]{1,0:T(8,128)(2,1)S(1)}, u32[]{:S(2)}, u32[]{:S(2)}) %collective-permute-start.11) | collective-permute-done | bytes 524320 | tf_op jit(solution)/shard_map/ppermute | solution.py:280
  182.9 0.8 copy-done.12
  183.6 4.1 %shard_map.98 = (bf16[256,1024]{1,0:T(8,128)(2,1)}, bf16[256,1024]{1,0:T(8,128)(2,1)}) custom-call(bf16[256,1024]{1,0:T(8,128)(2,1)} %bitcast.16, f32[256,512]{1,0:T(8,128)} %copy-done.2, f32[256,512]{1,0:T(8,128)} %copy-done.3, bf16[256,1024]{1,0:T(8,128)(2,1)} %copy-done.9, ...), custom_call_target="tpu_custom_call", output_to_operand_aliasing={{0}: (8, {}), {1}: (9, {})} | custom-call | flops 2621440 | bytes 3932160 | tf_op jit(solution)/shard_map/pallas_call | solution.py:228
  (31 shorter events, 0.1 us)
Async XLA Ops:
  0.6 42.0 %copy-start.1 = (bf16[1,1,256,1024]{3,2,1,0:T(8,128)(2,1)S(1)}, bf16[1,1,256,1024]{3,2,1,0:T(8,128)(2,1)}, u32[]{:S(2)}) copy-start(bf16[1,1,256,1024]{3,2,1,0:T(8,128)(2,1)} %param.9) | copy-start | bytes 1572868
  0.6 42.0 %copy-start = (bf16[1,1,256,1024]{3,2,1,0:T(8,128)(2,1)S(1)}, bf16[1,1,256,1024]{3,2,1,0:T(8,128)(2,1)}, u32[]{:S(2)}) copy-start(bf16[1,1,256,1024]{3,2,1,0:T(8,128)(2,1)} %param.8) | copy-start | bytes 1572868
  0.7 42.0 %copy-start.6 = (f32[128]{0:T(128)S(1)}, f32[128]{0:T(128)}, u32[]{:S(2)}) copy-start(f32[128]{0:T(128)} %param.10) | copy-start | bytes 1540
  0.7 42.0 %copy-start.7 = (bf16[1,128,8192]{2,1,0:T(8,128)(2,1)S(1)}, bf16[1,128,8192]{2,1,0:T(8,128)(2,1)}, u32[]{:S(2)}) copy-start(bf16[1,128,8192]{2,1,0:T(8,128)(2,1)} %param.6) | copy-start | bytes 6291460
  2.8 19.8 %collective-permute-start.7 = (bf16[256,1024]{1,0:T(8,128)(2,1)}, bf16[256,1024]{1,0:T(8,128)(2,1)}, u32[]{:S(2)}, u32[]{:S(2)}) collective-permute-start(bf16[256,1024]{1,0:T(8,128)(2,1)} %shard_map.94), channel_id=1, source_target_pairs={{0,32},{32,64},{64,96},{1,33},{33,65},{65,97},{2,34},{34,66},{66,9... | collective-permute-start | bytes 1572872 | tf_op jit(solution)/shard_map/ppermute | solution.py:270
  7.1 27.1 %collective-permute-start.6 = (bf16[256,1024]{1,0:T(8,128)(2,1)}, bf16[256,1024]{1,0:T(8,128)(2,1)}, u32[]{:S(2)}, u32[]{:S(2)}) collective-permute-start(bf16[256,1024]{1,0:T(8,128)(2,1)} %shard_map.94), channel_id=1, source_target_pairs={{0,24},{8,32},{32,56},{40,64},{64,88},{72,96},{96,120},{1,25},{9,3... | collective-permute-start | bytes 1572872 | tf_op jit(solution)/shard_map/ppermute | solution.py:270
  11.1 24.4 %collective-permute-start.5 = (bf16[256,1024]{1,0:T(8,128)(2,1)}, bf16[256,1024]{1,0:T(8,128)(2,1)}, u32[]{:S(2)}, u32[]{:S(2)}) collective-permute-start(bf16[256,1024]{1,0:T(8,128)(2,1)} %shard_map.94), channel_id=1, source_target_pairs={{0,16},{8,24},{16,32},{32,48},{40,56},{48,64},{64,80},{72,88},{80,... | collective-permute-start | bytes 1572872 | tf_op jit(solution)/shard_map/ppermute | solution.py:270
  13.2 29.4 %collective-permute-start.4 = (bf16[256,1024]{1,0:T(8,128)(2,1)}, bf16[256,1024]{1,0:T(8,128)(2,1)}, u32[]{:S(2)}, u32[]{:S(2)}) collective-permute-start(bf16[256,1024]{1,0:T(8,128)(2,1)} %shard_map.94), channel_id=1, source_target_pairs={{0,8},{8,16},{16,24},{24,32},{32,40},{40,48},{48,56},{56,64},{64,7... | collective-permute-start | bytes 1572872 | tf_op jit(solution)/shard_map/ppermute | solution.py:270
  18.7 50.5 %collective-permute-start.3 = (bf16[256,1024]{1,0:T(8,128)(2,1)}, bf16[256,1024]{1,0:T(8,128)(2,1)}, u32[]{:S(2)}, u32[]{:S(2)}) collective-permute-start(bf16[256,1024]{1,0:T(8,128)(2,1)} %shard_map.93), channel_id=1, source_target_pairs={{0,32},{32,64},{64,96},{1,33},{33,65},{65,97},{2,34},{34,66},{66,9... | collective-permute-start | bytes 1572872 | tf_op jit(solution)/shard_map/ppermute | solution.py:270
  22.6 47.9 %collective-permute-start.2 = (bf16[256,1024]{1,0:T(8,128)(2,1)}, bf16[256,1024]{1,0:T(8,128)(2,1)S(1)}, u32[]{:S(2)}, u32[]{:S(2)}) collective-permute-start(bf16[256,1024]{1,0:T(8,128)(2,1)} %shard_map.93), channel_id=1, source_target_pairs={{0,24},{8,32},{32,56},{40,64},{64,88},{72,96},{96,120},{1,25},{9,3... | collective-permute-start | bytes 1572872 | tf_op jit(solution)/shard_map/ppermute | solution.py:270
  34.1 37.8 %collective-permute-start.1 = (bf16[256,1024]{1,0:T(8,128)(2,1)}, bf16[256,1024]{1,0:T(8,128)(2,1)S(1)}, u32[]{:S(2)}, u32[]{:S(2)}) collective-permute-start(bf16[256,1024]{1,0:T(8,128)(2,1)} %shard_map.93), channel_id=1, source_target_pairs={{0,16},{8,24},{16,32},{32,48},{40,56},{48,64},{64,80},{72,88},{80,... | collective-permute-start | bytes 1572872 | tf_op jit(solution)/shard_map/ppermute | solution.py:270
  35.5 36.5 %collective-permute-start = (bf16[256,1024]{1,0:T(8,128)(2,1)}, bf16[256,1024]{1,0:T(8,128)(2,1)S(1)}, u32[]{:S(2)}, u32[]{:S(2)}) collective-permute-start(bf16[256,1024]{1,0:T(8,128)(2,1)} %shard_map.93), channel_id=1, source_target_pairs={{0,8},{8,16},{16,24},{24,32},{32,40},{40,48},{48,56},{56,64},{64,7... | collective-permute-start | bytes 1572872 | tf_op jit(solution)/shard_map/ppermute | solution.py:270
  42.6 1.6 copy-start.8
  66.3 0.8 copy-start.4
  67.1 0.8 copy-start.5
  67.9 63.0 %collective-permute-start.12 = (bf16[256,1024]{1,0:T(8,128)(2,1)S(1)}, bf16[256,1024]{1,0:T(8,128)(2,1)S(1)}, u32[]{:S(2)}, u32[]{:S(2)}) collective-permute-start(bf16[256,1024]{1,0:T(8,128)(2,1)S(1)} %get-tuple-element.34), channel_id=1, source_target_pairs={{8,0},{16,8},{24,16},{32,24},{40,32},{48,40},{56,48},{64,56},{72,6... | collective-permute-start | bytes 1572872 | tf_op jit(solution)/shard_map/ppermute | solution.py:280
  69.2 63.0 %collective-permute-start.13 = (bf16[256,1024]{1,0:T(8,128)(2,1)S(1)}, bf16[256,1024]{1,0:T(8,128)(2,1)S(1)}, u32[]{:S(2)}, u32[]{:S(2)}) collective-permute-start(bf16[256,1024]{1,0:T(8,128)(2,1)S(1)} %get-tuple-element.35), channel_id=1, source_target_pairs={{16,0},{24,8},{32,16},{48,32},{56,40},{64,48},{80,64},{88,72},{96,... | collective-permute-start | bytes 1572872 | tf_op jit(solution)/shard_map/ppermute | solution.py:280
  70.5 63.0 %collective-permute-start.14 = (bf16[256,1024]{1,0:T(8,128)(2,1)S(1)}, bf16[256,1024]{1,0:T(8,128)(2,1)S(1)}, u32[]{:S(2)}, u32[]{:S(2)}) collective-permute-start(bf16[256,1024]{1,0:T(8,128)(2,1)S(1)} %get-tuple-element.36), channel_id=1, source_target_pairs={{24,0},{32,8},{56,32},{64,40},{88,64},{96,72},{120,96},{25,1},{33,... | collective-permute-start | bytes 1572872 | tf_op jit(solution)/shard_map/ppermute | solution.py:280
  94.1 0.8 copy-start.2
  94.9 0.8 copy-start.3
  95.7 1.1 collective-permute-start.16
  96.8 3.5 %collective-permute-start.17 = (f32[1,128]{1,0:T(1,128)S(1)}, f32[1,128]{1,0:T(1,128)S(1)}, u32[]{:S(2)}, u32[]{:S(2)}) collective-permute-start(f32[1,128]{1,0:T(1,128)S(1)} %add.30), channel_id=1, source_target_pairs={{0,2},{1,3},{2,0},{3,1},{4,6},{5,7},{6,4},{7,5},{8,10},{9,11},{10,... | collective-permute-start | bytes 1544 | tf_op jit(solution)/shard_map/ppermute | solution.py:255
  100.4 5.0 %collective-permute-start.18 = (f32[1,128]{1,0:T(1,128)S(1)}, f32[1,128]{1,0:T(1,128)S(1)}, u32[]{:S(2)}, u32[]{:S(2)}) collective-permute-start(f32[1,128]{1,0:T(1,128)S(1)} %add.31), channel_id=1, source_target_pairs={{0,4},{1,5},{2,6},{3,7},{4,0},{5,1},{6,2},{7,3},{8,12},{9,13},{10,... | collective-permute-start | bytes 1544 | tf_op jit(solution)/shard_map/ppermute | solution.py:255
  105.4 3.5 %collective-permute-start.19 = (f32[1,128]{1,0:T(1,128)S(1)}, f32[1,128]{1,0:T(1,128)S(1)}, u32[]{:S(2)}, u32[]{:S(2)}) collective-permute-start(f32[1,128]{1,0:T(1,128)S(1)} %add.32), channel_id=1, source_target_pairs={{0,8},{8,0},{16,24},{24,16},{32,40},{40,32},{48,56},{56,48},{64,72... | collective-permute-start | bytes 1544 | tf_op jit(solution)/shard_map/ppermute | solution.py:255
  109.0 5.0 %collective-permute-start.20 = (f32[1,128]{1,0:T(1,128)S(1)}, f32[1,128]{1,0:T(1,128)S(1)}, u32[]{:S(2)}, u32[]{:S(2)}) collective-permute-start(f32[1,128]{1,0:T(1,128)S(1)} %add.33), channel_id=1, source_target_pairs={{0,16},{8,24},{16,0},{24,8},{32,48},{40,56},{48,32},{56,40},{64,80... | collective-permute-start | bytes 1544 | tf_op jit(solution)/shard_map/ppermute | solution.py:255
  114.0 9.1 %collective-permute-start.21 = (f32[1,128]{1,0:T(1,128)S(1)}, f32[1,128]{1,0:T(1,128)S(1)}, u32[]{:S(2)}, u32[]{:S(2)}) collective-permute-start(f32[1,128]{1,0:T(1,128)S(1)} %add.34), channel_id=1, source_target_pairs={{0,32},{8,40},{16,48},{24,56},{32,0},{40,8},{48,16},{56,24},{64,96... | collective-permute-start | bytes 1544 | tf_op jit(solution)/shard_map/ppermute | solution.py:255
  123.1 6.4 %collective-permute-start.22 = (f32[1,128]{1,0:T(1,128)S(1)}, f32[1,128]{1,0:T(1,128)S(1)}, u32[]{:S(2)}, u32[]{:S(2)}) collective-permute-start(f32[1,128]{1,0:T(1,128)S(1)} %add.35), channel_id=1, source_target_pairs={{0,64},{8,72},{16,80},{24,88},{32,96},{40,104},{48,112},{56,120},{... | collective-permute-start | bytes 1544 | tf_op jit(solution)/shard_map/ppermute | solution.py:255
  128.0 16.7 %collective-permute-start.15 = (bf16[256,1024]{1,0:T(8,128)(2,1)S(1)}, bf16[256,1024]{1,0:T(8,128)(2,1)S(1)}, u32[]{:S(2)}, u32[]{:S(2)}) collective-permute-start(bf16[256,1024]{1,0:T(8,128)(2,1)S(1)} %get-tuple-element.37), channel_id=1, source_target_pairs={{32,0},{64,32},{96,64},{33,1},{65,33},{97,65},{34,2},{66,34},{98,6... | collective-permute-start | bytes 1572872 | tf_op jit(solution)/shard_map/ppermute | solution.py:280
  129.5 20.2 %collective-permute-start.8 = (bf16[256,1024]{1,0:T(8,128)(2,1)}, bf16[256,1024]{1,0:T(8,128)(2,1)S(1)}, u32[]{:S(2)}, u32[]{:S(2)}) collective-permute-start(bf16[256,1024]{1,0:T(8,128)(2,1)} %get-tuple-element.28), channel_id=1, source_target_pairs={{8,0},{16,8},{24,16},{32,24},{40,32},{48,40},{56,48},{64,56},{72,6... | collective-permute-start | bytes 1572872 | tf_op jit(solution)/shard_map/ppermute | solution.py:280
  130.8 13.9 %copy-start.13 = (bf16[256,1024]{1,0:T(8,128)(2,1)}, bf16[256,1024]{1,0:T(8,128)(2,1)S(1)}, u32[]{:S(2)}) copy-start(bf16[256,1024]{1,0:T(8,128)(2,1)S(1)} %collective-permute-done.12.rest_0_) | copy-start | bytes 1572868
  130.8 18.9 %collective-permute-start.9 = (bf16[256,1024]{1,0:T(8,128)(2,1)}, bf16[256,1024]{1,0:T(8,128)(2,1)S(1)}, u32[]{:S(2)}, u32[]{:S(2)}) collective-permute-start(bf16[256,1024]{1,0:T(8,128)(2,1)} %get-tuple-element.29), channel_id=1, source_target_pairs={{16,0},{24,8},{32,16},{48,32},{56,40},{64,48},{80,64},{88,72},{96,... | collective-permute-start | bytes 1572872 | tf_op jit(solution)/shard_map/ppermute | solution.py:280
  132.2 12.6 %copy-start.14 = (bf16[256,1024]{1,0:T(8,128)(2,1)}, bf16[256,1024]{1,0:T(8,128)(2,1)S(1)}, u32[]{:S(2)}) copy-start(bf16[256,1024]{1,0:T(8,128)(2,1)S(1)} %collective-permute-done.13.rest_1_) | copy-start | bytes 1572868
  132.2 21.3 %collective-permute-start.10 = (bf16[256,1024]{1,0:T(8,128)(2,1)}, bf16[256,1024]{1,0:T(8,128)(2,1)S(1)}, u32[]{:S(2)}, u32[]{:S(2)}) collective-permute-start(bf16[256,1024]{1,0:T(8,128)(2,1)} %get-tuple-element.30), channel_id=1, source_target_pairs={{24,0},{32,8},{56,32},{64,40},{88,64},{96,72},{120,96},{25,1},{33,... | collective-permute-start | bytes 1572872 | tf_op jit(solution)/shard_map/ppermute | solution.py:280
  133.5 11.3 %copy-start.15 = (bf16[256,1024]{1,0:T(8,128)(2,1)}, bf16[256,1024]{1,0:T(8,128)(2,1)S(1)}, u32[]{:S(2)}) copy-start(bf16[256,1024]{1,0:T(8,128)(2,1)S(1)} %collective-permute-done.14.rest_2_) | copy-start | bytes 1572868
  133.5 49.4 %collective-permute-start.11 = (bf16[256,1024]{1,0:T(8,128)(2,1)}, bf16[256,1024]{1,0:T(8,128)(2,1)S(1)}, u32[]{:S(2)}, u32[]{:S(2)}) collective-permute-start(bf16[256,1024]{1,0:T(8,128)(2,1)} %get-tuple-element.31), channel_id=1, source_target_pairs={{32,0},{64,32},{96,64},{33,1},{65,33},{97,65},{34,2},{66,34},{98,6... | collective-permute-start | bytes 1572872 | tf_op jit(solution)/shard_map/ppermute | solution.py:280
  144.8 0.8 copy-start.16
  149.7 33.1 %copy-start.9 = (bf16[256,1024]{1,0:T(8,128)(2,1)}, bf16[256,1024]{1,0:T(8,128)(2,1)S(1)}, u32[]{:S(2)}) copy-start(bf16[256,1024]{1,0:T(8,128)(2,1)S(1)} %collective-permute-done.8.rest_0_) | copy-start | bytes 1572868
  149.7 33.1 %copy-start.10 = (bf16[256,1024]{1,0:T(8,128)(2,1)}, bf16[256,1024]{1,0:T(8,128)(2,1)S(1)}, u32[]{:S(2)}) copy-start(bf16[256,1024]{1,0:T(8,128)(2,1)S(1)} %collective-permute-done.9.rest_1_) | copy-start | bytes 1572868
  153.5 29.4 %copy-start.11 = (bf16[256,1024]{1,0:T(8,128)(2,1)}, bf16[256,1024]{1,0:T(8,128)(2,1)S(1)}, u32[]{:S(2)}) copy-start(bf16[256,1024]{1,0:T(8,128)(2,1)S(1)} %collective-permute-done.10.rest_2_) | copy-start | bytes 1572868
  182.8 0.8 copy-start.12

commit v2 on v1

--- a/solution.py
+++ b/solution.py
@@ -9,7 +9,7 @@
 
 DOC_IMG = 4
 SPAN = DOC_IMG + 1
-CHUNKS = 2
+HEADS = (4, 4)
 HD = 128
 MASKED = -1e30
 SCALE = HD**-0.5
@@ -17,7 +17,7 @@
 NT = (((1,), (1,)), ((), ()))
 TN = (((0,), (0,)), ((), ()))
 NN = (((1,), (0,)), ((), ()))
-VMEM_LIMIT = 40 * 2**20
+VMEM_LIMIT = 60 * 2**20
 
 
 def dot(left, right, dims):
@@ -39,12 +39,13 @@
 
 def pack(key_raw, values, chunk):
     rows, width = key_raw.shape
-    part = width // CHUNKS
+    first, heads = sum(HEADS[:chunk]), HEADS[chunk]
+    part = heads * HD
     return pl.pallas_call(
         pack_kernel,
-        grid=(1,),
-        in_specs=[pl.BlockSpec((rows, part), lambda i: (0, chunk))] * 2,
-        out_specs=pl.BlockSpec((rows, 2 * part), lambda i: (0, 0)),
+        grid=(heads // 2,),
+        in_specs=[pl.BlockSpec((rows, 2 * HD), lambda i: (0, first // 2 + i))] * 2,
+        out_specs=pl.BlockSpec((rows, 4 * HD), lambda i: (0, i)),
         out_shape=jax.ShapeDtypeStruct((rows, 2 * part), key_raw.dtype),
         cost_estimate=pl.CostEstimate(flops=0, bytes_accessed=8 * rows * part, transcendentals=0),
     )(key_raw, values)
@@ -152,8 +153,7 @@
     rows = key_raw.shape[0]
     kv_heads = key_raw.shape[1] // HD
     group = width // HD // kv_heads
-    heads = kv_heads // CHUNKS
-    first = chunk * heads
+    first, heads = sum(HEADS[:chunk]), HEADS[chunk]
     wide = pl.BlockSpec((tokens, group * HD), lambda h: (0, first + h))
     own = pl.BlockSpec((rows, HD), lambda h: (0, first + h))
     part = pl.BlockSpec((rows, 2 * HD), lambda h: (0, h))
@@ -195,31 +195,38 @@
     return outs[0], outs[1], outs[2], outs[3 : 3 + DOC_IMG], outs[3 + DOC_IMG]
 
 
-def finish_kernel(key_ref, own_k, own_v, *rest, aliased):
+def finish_kernel(meta, key_ref, own_k, own_v, *rest, aliased):
     back, gain_ref, rest = rest[:DOC_IMG], rest[DOC_IMG], rest[DOC_IMG + 1 :]
     if aliased:
         rest = rest[2:]
     gk_ref, gv_ref = rest
+    shard = meta[0]
     unit, inv_rms = unit_norm(key_ref[...])
     dk, dv = own_k[...], own_v[...]
-    for ref in back:
-        dk = dk + ref[:, :HD].astype(jnp.float32)
-        dv = dv + ref[:, HD:].astype(jnp.float32)
+    for distance, ref in enumerate(back, 1):
+        dk_part = ref[:, :HD].astype(jnp.float32)
+        dv_part = ref[:, HD:].astype(jnp.float32)
+        if distance < DOC_IMG:
+            held = shard + distance < DOC_IMG
+            dk_part = jnp.where(held, dk_part, 0.0)
+            dv_part = jnp.where(held, dv_part, 0.0)
+        dk = dk + dk_part
+        dv = dv + dv_part
     scaled = dk * gain_ref[...]
     inner = jnp.mean(scaled * unit, -1, keepdims=True)
     gk_ref[...] = (inv_rms * (scaled - unit * inner)).astype(gk_ref.dtype)
     gv_ref[...] = dv.astype(gv_ref.dtype)
 
 
-def finish(key_raw, own_k, own_v, back, gain, done, chunk):
+def finish(meta, key_raw, own_k, own_v, back, gain, done, chunk):
     rows, width = key_raw.shape
-    heads = width // HD // CHUNKS
-    first = chunk * heads
+    first, heads = sum(HEADS[:chunk]), HEADS[chunk]
     local = pl.BlockSpec((rows, HD), lambda h: (0, h))
     part = pl.BlockSpec((rows, 2 * HD), lambda h: (0, h))
     placed = pl.BlockSpec((rows, HD), lambda h: (0, first + h))
-    args = [key_raw, own_k, own_v, *back, gain]
-    in_specs = [placed, local, local] + [part] * DOC_IMG + [pl.BlockSpec((1, HD), lambda h: (0, 0))]
+    args = [meta, key_raw, own_k, own_v, *back, gain]
+    in_specs = [pl.BlockSpec(memory_space=pltpu.SMEM), placed, local, local]
+    in_specs += [part] * DOC_IMG + [pl.BlockSpec((1, HD), lambda h: (0, 0))]
     aliases = {}
     if done is not None:
         aliases = {len(args): 0, len(args) + 1: 1}
@@ -247,13 +254,23 @@
     return pairs
 
 
-def all_sum(value):
-    for axis in ("dp", "ctx"):
-        count = lax.axis_size(axis)
-        step = 1
-        while step < count:
-            value = value + lax.ppermute(value, axis, [(i, i ^ step) for i in range(count)])
-            step *= 2
+def ring_pairs(count, distance):
+    pairs = []
+    for reader in range(count):
+        place = reader % DOC_IMG
+        if place >= distance or (place == 0 and reader):
+            pairs.append((reader, reader - place + (place - distance) % DOC_IMG))
+    return pairs
+
+
+def before_pairs(count):
+    return [(reader, reader - DOC_IMG) for reader in range(DOC_IMG, count)]
+
+
+def all_sum(value, axis, steps):
+    for step in steps:
+        pairs = [(i, i ^ step) for i in range(lax.axis_size(axis))]
+        value = value + lax.ppermute(value, axis, pairs)
     return value
 
 
@@ -262,30 +279,41 @@
     queries, grad_out = queries[0], grad_out[0]
     key_raw, values = key_raw[0, 0], values[0, 0]
     gain = key_gain[None]
-    meta = jnp.stack([lax.axis_index("ctx") % DOC_IMG, image_pos[0, 0]]).astype(jnp.int32)
+    shard = lax.axis_index("ctx") % DOC_IMG
+    meta = jnp.stack([shard, image_pos[0, 0]]).astype(jnp.int32)
     pairs = [reader_pairs(count, distance) for distance in range(1, SPAN)]
     recv = []
-    for chunk in range(CHUNKS):
+    for chunk in range(len(HEADS)):
         packed = pack(key_raw, values, chunk)
         recv.append([lax.ppermute(packed, "ctx", to) for to in pairs])
-    dq = None
+    dq = done = None
     gain_part = 0.0
-    held = []
-    for chunk in range(CHUNKS):
+    own, back = [], []
+    for chunk in range(len(HEADS)):
         dq, own_k, own_v, parts, part = attend(
             meta, queries, grad_out, key_raw, values, recv[chunk], gain, dq, chunk
         )
         gain_part = gain_part + part
-        back = [
-            lax.ppermute(value, "ctx", [(reader, owner) for owner, reader in to])
-            for value, to in zip(parts, pairs)
-        ]
-        held.append((own_k, own_v, back))
-    grad_gain = all_sum(gain_part)
-    done = None
-    for chunk, (own_k, own_v, back) in enumerate(held):
-        done = finish(key_raw, own_k, own_v, back, gain, done, chunk)
-    return dq[None], done[0][None, None], done[1][None, None], grad_gain[0]
+        own.append((own_k, own_v))
+        back.append(
+            [
+                lax.ppermute(parts[distance - 1], "ctx", ring_pairs(count, distance))
+                for distance in range(1, DOC_IMG)
+            ]
+        )
+        handed = lax.select_n(shard, parts[-1], *back[chunk][::-1])
+        if chunk == len(HEADS) - 1:
+            gain_part = all_sum(gain_part, "dp", (1, 2, 4))
+            gain_part = all_sum(gain_part, "ctx", (4, 8))
+            if done is None:
+                handed, gain_part = lax.optimization_barrier((handed, gain_part))
+            else:
+                handed, gain_part, done = lax.optimization_barrier((handed, gain_part, done))
+        back[chunk].append(lax.ppermute(handed, "ctx", before_pairs(count)))
+        if chunk == len(HEADS) - 1:
+            gain_part = all_sum(gain_part, "ctx", (1, 2))
+        done = finish(meta, key_raw, *own[chunk], back[chunk], gain, done, chunk)
+    return dq[None], done[0][None, None], done[1][None, None], gain_part[0]
 
 
 def solution(mesh):

time: 189 us -> 157 us (0.83)
  waiting for transfers between devices: 65.7 us -> 31.5 us
  starting transfers between devices: 57 us -> 61.2 us
  local copies, waits for them, and re-layouts: 6.42 us -> 2.43 us
    ppermute x15, waiting for transfers between devices: 55.9 us -> 21.5 us  [the longest x7 14.4 us: all_sum(): value = value + lax.ppermute(value, axis, pairs)]
    ppermute x15, starting transfers between devices: 29.7 us -> 34 us  [the longest x7 23.4 us: all_sum(): value = value + lax.ppermute(value, axis, pairs)]
    unnamed x34 -> x36, local copies, waits for them, and re-layouts: 6.42 us -> 2.43 us
  transfers between devices with their start and end apart: 23 -> 23, of which waited for: 11 -> 9; matrix products, arithmetic and copies ran while one was open for 0% -> 2% of each run, Pallas kernels for 27% -> 30%
where the time goes in v2:
time: 157 us; the launch traced here: 156 us
  starting transfers between devices  61.2 us (39%)
  Pallas kernels  56.4 us (36%)
  waiting for transfers between devices  31.5 us (20%)
  local copies, waits for them, and re-layouts  2.43 us (2%)
  other arithmetic  2.39 us (2%)
  between operations  1.72 us (1%)
    pallas_call x2, Pallas kernels, attend(): pl.pallas_call(functools.partial(attend_kernel, aliased=dq is not None),...  44.3 us
    ppermute x8, starting transfers between devices, shards(): recv.append([lax.ppermute(packed, 'ctx', to) for to in pairs])  27.2 us
    ppermute x7, starting transfers between devices, all_sum(): value = value + lax.ppermute(value, axis, pairs)  23.4 us
    ppermute x7, waiting for transfers between devices, all_sum(): value = value + lax.ppermute(value, axis, pairs)  14.4 us
    ppermute x8, waiting for transfers between devices, shards(): recv.append([lax.ppermute(packed, 'ctx', to) for to in pairs])  10 us
    pallas_call x2, Pallas kernels, finish(): pl.pallas_call(functools.partial(finish_kernel, aliased=done is not None)...  8.34 us
    ppermute x6, starting transfers between devices, shards(): lax.ppermute(parts[distance - 1], 'ctx', ring_pairs(count, distance))  8.06 us
    ppermute x2, waiting for transfers between devices, shards(): back[chunk].append(lax.ppermute(handed, 'ctx', before_pairs(count)))  7.1 us
  transfers between devices with their start and end apart: 23, of which 9 were waited for; matrix products, arithmetic and copies ran while one was open for 2% of the time, Pallas kernels for 30%

profile of v2, /device:TPU:0, one launch (start us, length us, event | category | flops | bytes accessed | tf_op | source)
XLA Modules:
  0.0 155.6 jit_solution(16623449054820340000)
XLA Ops:
  0.6 1.9 %shard_map.94 = bf16[256,1024]{1,0:T(8,128)(2,1)} custom-call(bf16[256,1024]{1,0:T(8,128)(2,1)} %bitcast.13, bf16[256,1024]{1,0:T(8,128)(2,1)} %bitcast.19), custom_call_target="tpu_custom_call" | custom-call | bytes 1048576 | tf_op jit(solution)/shard_map/pallas_call | solution.py:44
  2.5 3.5 %collective-permute-start.7 = (bf16[256,1024]{1,0:T(8,128)(2,1)}, bf16[256,1024]{1,0:T(8,128)(2,1)S(1)}, u32[]{:S(2)}, u32[]{:S(2)}) collective-permute-start(bf16[256,1024]{1,0:T(8,128)(2,1)} %shard_map.94), channel_id=1, source_target_pairs={{0,32},{32,64},{64,96},{1,33},{33,65},{65,97},{2,34},{34,66},{66,9... | collective-permute-start | bytes 1572872 | tf_op jit(solution)/shard_map/ppermute | solution.py:288
  6.0 3.2 %collective-permute-start.6 = (bf16[256,1024]{1,0:T(8,128)(2,1)}, bf16[256,1024]{1,0:T(8,128)(2,1)S(1)}, u32[]{:S(2)}, u32[]{:S(2)}) collective-permute-start(bf16[256,1024]{1,0:T(8,128)(2,1)} %shard_map.94), channel_id=1, source_target_pairs={{0,24},{8,32},{32,56},{40,64},{64,88},{72,96},{96,120},{1,25},{9,3... | collective-permute-start | bytes 1572872 | tf_op jit(solution)/shard_map/ppermute | solution.py:288
  9.2 1.3 collective-permute-start.5
  10.6 3.6 %collective-permute-start.4 = (bf16[256,1024]{1,0:T(8,128)(2,1)}, bf16[256,1024]{1,0:T(8,128)(2,1)S(1)}, u32[]{:S(2)}, u32[]{:S(2)}) collective-permute-start(bf16[256,1024]{1,0:T(8,128)(2,1)} %shard_map.94), channel_id=1, source_target_pairs={{0,8},{8,16},{16,24},{24,32},{32,40},{40,48},{48,56},{56,64},{64,7... | collective-permute-start | bytes 1572872 | tf_op jit(solution)/shard_map/ppermute | solution.py:288
  14.1 1.9 %shard_map.93 = bf16[256,1024]{1,0:T(8,128)(2,1)} custom-call(bf16[256,1024]{1,0:T(8,128)(2,1)} %bitcast.14, bf16[256,1024]{1,0:T(8,128)(2,1)} %bitcast.20), custom_call_target="tpu_custom_call" | custom-call | bytes 1048576 | tf_op jit(solution)/shard_map/pallas_call | solution.py:44
  16.0 3.1 %collective-permute-start.3 = (bf16[256,1024]{1,0:T(8,128)(2,1)}, bf16[256,1024]{1,0:T(8,128)(2,1)S(1)}, u32[]{:S(2)}, u32[]{:S(2)}) collective-permute-start(bf16[256,1024]{1,0:T(8,128)(2,1)} %shard_map.93), channel_id=1, source_target_pairs={{0,32},{32,64},{64,96},{1,33},{33,65},{65,97},{2,34},{34,66},{66,9... | collective-permute-start | bytes 1572872 | tf_op jit(solution)/shard_map/ppermute | solution.py:288
  19.8 0.7 pad_add_fusion.meta
  20.5 0.0 collective-permute-done.7.rest_3_
  20.5 2.6 %collective-permute-start.2 = (bf16[256,1024]{1,0:T(8,128)(2,1)}, bf16[256,1024]{1,0:T(8,128)(2,1)S(1)}, u32[]{:S(2)}, u32[]{:S(2)}) collective-permute-start(bf16[256,1024]{1,0:T(8,128)(2,1)} %shard_map.93), channel_id=1, source_target_pairs={{0,24},{8,32},{32,56},{40,64},{64,88},{72,96},{96,120},{1,25},{9,3... | collective-permute-start | bytes 1572872 | tf_op jit(solution)/shard_map/ppermute | solution.py:288
  23.1 10.0 %collective-permute-done.6.rest_2_ = bf16[256,1024]{1,0:T(8,128)(2,1)S(1)} collective-permute-done((bf16[256,1024]{1,0:T(8,128)(2,1)}, bf16[256,1024]{1,0:T(8,128)(2,1)S(1)}, u32[]{:S(2)}, u32[]{:S(2)}) %collective-permute-start.6) | collective-permute-done | bytes 524320 | tf_op jit(solution)/shard_map/ppermute | solution.py:288
  33.1 2.1 %collective-permute-start.1 = (bf16[256,1024]{1,0:T(8,128)(2,1)}, bf16[256,1024]{1,0:T(8,128)(2,1)}, u32[]{:S(2)}, u32[]{:S(2)}) collective-permute-start(bf16[256,1024]{1,0:T(8,128)(2,1)} %shard_map.93), channel_id=1, source_target_pairs={{0,16},{8,24},{16,32},{32,48},{40,56},{48,64},{64,80},{72,88},{80,... | collective-permute-start | bytes 1572872 | tf_op jit(solution)/shard_map/ppermute | solution.py:288
  35.2 0.0 collective-permute-done.5.rest_1_
  35.2 7.8 %collective-permute-start = (bf16[256,1024]{1,0:T(8,128)(2,1)}, bf16[256,1024]{1,0:T(8,128)(2,1)}, u32[]{:S(2)}, u32[]{:S(2)}) collective-permute-start(bf16[256,1024]{1,0:T(8,128)(2,1)} %shard_map.93), channel_id=1, source_target_pairs={{0,8},{8,16},{16,24},{24,32},{32,40},{40,48},{48,56},{56,64},{64,7... | collective-permute-start | bytes 1572872 | tf_op jit(solution)/shard_map/ppermute | solution.py:288
  42.9 0.0 collective-permute-done.4.rest_0_
  43.0 0.8 copy-done.14
  43.7 22.1 %shard_map.95 = (bf16[128,8192]{1,0:T(8,128)(2,1)}, f32[256,512]{1,0:T(8,128)}, f32[256,512]{1,0:T(8,128)}, bf16[256,1024]{1,0:T(8,128)(2,1)}, bf16[256,1024]{1,...) custom-call(s32[2]{0:T(128)} %pad_add_fusion.meta, ...), custom_call_target="tpu_custom_call" | custom-call | flops 6710886400 | bytes 18874368 | tf_op jit(solution)/shard_map/pallas_call | solution.py:171
  65.8 1.3 collective-permute-start.16
  67.1 0.0 collective-permute-done.3.rest_3_
  67.1 1.3 collective-permute-start.17
  68.4 0.0 collective-permute-done.2.rest_2_
  68.5 0.0 copy-start.15
  68.5 1.5 collective-permute-start.18
  69.9 0.0 collective-permute-done.1.rest_1_
  70.0 0.0 collective-permute-done.rest_0_
  70.0 0.0 copy-done.15
  70.0 0.0 copy-done.10
  70.0 0.0 copy-start.9
  70.0 22.2 %shard_map.96 = (bf16[128,8192]{1,0:T(8,128)(2,1)}, f32[256,512]{1,0:T(8,128)}, f32[256,512]{1,0:T(8,128)}, bf16[256,1024]{1,0:T(8,128)(2,1)}, bf16[256,1024]{1,...) custom-call(s32[2]{0:T(128)} %pad_add_fusion.meta, ...), custom_call_target="tpu_custom_call", output_to_operand_aliasing={{0}: (10, {})} | custom-call | flops 6710886400 | bytes 18874368 | tf_op jit(solution)/shard_map/pallas_call | solution.py:171
  92.2 0.0 copy-start.16
  92.2 1.4 collective-permute-start.8
  93.7 1.3 collective-permute-start.9
  95.0 0.0 collective-permute-done.16.rest_0_
  95.0 1.3 collective-permute-start.10
  96.3 0.0 collective-permute-done.17.rest_1_
  96.3 0.0 collective-permute-done.18.rest_2_
  96.3 0.1 select_select_fusion
  96.5 1.3 collective-permute-start.19
  97.8 0.1 collective-permute-start.11
  97.9 1.1 collective-permute-done.11
  99.0 1.6 %collective-permute-start.12 = (f32[1,128]{1,0:T(1,128)S(1)}, f32[1,128]{1,0:T(1,128)S(1)}, u32[]{:S(2)}, u32[]{:S(2)}) collective-permute-start(f32[1,128]{1,0:T(1,128)S(1)} %add.30), channel_id=1, source_target_pairs={{0,2},{1,3},{2,0},{3,1},{4,6},{5,7},{6,4},{7,5},{8,10},{9,11},{10,... | collective-permute-start | bytes 1544 | tf_op jit(solution)/shard_map/ppermute | solution.py:273
  100.6 2.0 %collective-permute-done.12 = f32[1,128]{1,0:T(1,128)S(1)} collective-permute-done((f32[1,128]{1,0:T(1,128)S(1)}, f32[1,128]{1,0:T(1,128)S(1)}, u32[]{:S(2)}, u32[]{:S(2)}) %collective-permute-start.12) | collective-permute-done | bytes 544 | tf_op jit(solution)/shard_map/ppermute | solution.py:273
  102.5 3.2 %collective-permute-start.13 = (f32[1,128]{1,0:T(1,128)S(1)}, f32[1,128]{1,0:T(1,128)S(1)}, u32[]{:S(2)}, u32[]{:S(2)}) collective-permute-start(f32[1,128]{1,0:T(1,128)S(1)} %add.31), channel_id=1, source_target_pairs={{0,4},{1,5},{2,6},{3,7},{4,0},{5,1},{6,2},{7,3},{8,12},{9,13},{10,... | collective-permute-start | bytes 1544 | tf_op jit(solution)/shard_map/ppermute | solution.py:273
  105.7 1.8 %collective-permute-done.13 = f32[1,128]{1,0:T(1,128)S(1)} collective-permute-done((f32[1,128]{1,0:T(1,128)S(1)}, f32[1,128]{1,0:T(1,128)S(1)}, u32[]{:S(2)}, u32[]{:S(2)}) %collective-permute-start.13) | collective-permute-done | bytes 544 | tf_op jit(solution)/shard_map/ppermute | solution.py:273
  107.6 12.2 %collective-permute-start.14 = (f32[1,128]{1,0:T(1,128)S(1)}, f32[1,128]{1,0:T(1,128)S(1)}, u32[]{:S(2)}, u32[]{:S(2)}) collective-permute-start(f32[1,128]{1,0:T(1,128)S(1)} %add.32), channel_id=1, source_target_pairs={{0,32},{8,40},{16,48},{24,56},{32,0},{40,8},{48,16},{56,24},{64,96... | collective-permute-start | bytes 1544 | tf_op jit(solution)/shard_map/ppermute | solution.py:273
  119.8 1.5 collective-permute-done.14
  121.3 4.1 %collective-permute-start.15 = (f32[1,128]{1,0:T(1,128)S(1)}, f32[1,128]{1,0:T(1,128)S(1)}, u32[]{:S(2)}, u32[]{:S(2)}) collective-permute-start(f32[1,128]{1,0:T(1,128)S(1)} %add.33), channel_id=1, source_target_pairs={{0,64},{8,72},{16,80},{24,88},{32,96},{40,104},{48,112},{56,120},{... | collective-permute-start | bytes 1544 | tf_op jit(solution)/shard_map/ppermute | solution.py:273
  125.4 1.5 collective-permute-done.15
  126.9 0.0 collective-permute-done.8.rest_0_
  126.9 0.0 collective-permute-done.9.rest_1_
  126.9 0.0 collective-permute-done.10.rest_2_
  127.0 1.1 select_select_fusion.1
  128.1 0.0 collective-permute-done.19.rest_3_
  128.1 0.8 copy-done.8
  128.9 4.2 %shard_map.97 = (bf16[256,1024]{1,0:T(8,128)(2,1)}, bf16[256,1024]{1,0:T(8,128)(2,1)}) custom-call(s32[2]{0:T(128)} %pad_add_fusion.meta, bf16[256,1024]{1,0:T(8,128)(2,1)} %bitcast.17, f32[256,512]{1,0:T(8,128)} %get-tuple-element.38.own_k, f32[256,512]{1,0:T(8,128)} %get-tuple-element.39.own_v, bf16[256,1024]{1,0:T(8,128)(2,1)} %copy-done.3, ...), custom_call_target="tpu_custom_call" | custom-call | flops 2621440 | bytes 3932160 | tf_op jit(solution)/shard_map/pallas_call | solution.py:235
  133.1 1.3 collective-permute-start.20
  134.4 0.1 collective-permute-start.21
  134.5 3.5 %collective-permute-done.21 = f32[1,128]{1,0:T(1,128)S(1)} collective-permute-done((f32[1,128]{1,0:T(1,128)S(1)}, f32[1,128]{1,0:T(1,128)S(1)}, u32[]{:S(2)}, u32[]{:S(2)}) %collective-permute-start.21) | collective-permute-done | bytes 544 | tf_op jit(solution)/shard_map/ppermute | solution.py:273
  138.0 2.2 %collective-permute-start.22 = (f32[1,128]{1,0:T(1,128)S(1)}, f32[1,128]{1,0:T(1,128)S(1)}, u32[]{:S(2)}, u32[]{:S(2)}) collective-permute-start(f32[1,128]{1,0:T(1,128)S(1)} %add.35), channel_id=1, source_target_pairs={{0,16},{8,24},{16,0},{24,8},{32,48},{40,56},{48,32},{56,40},{64,80... | collective-permute-start | bytes 1544 | tf_op jit(solution)/shard_map/ppermute | solution.py:273
  140.2 2.9 %collective-permute-done.22 = f32[1,128]{1,0:T(1,128)S(1)} collective-permute-done((f32[1,128]{1,0:T(1,128)S(1)}, f32[1,128]{1,0:T(1,128)S(1)}, u32[]{:S(2)}, u32[]{:S(2)}) %collective-permute-start.22) | collective-permute-done | bytes 544 | tf_op jit(solution)/shard_map/ppermute | solution.py:273
  143.0 0.5 add_bitcast_fusion
  143.6 7.1 %collective-permute-done.20.rest_3_ = bf16[256,1024]{1,0:T(8,128)(2,1)S(1)} collective-permute-done((bf16[256,1024]{1,0:T(8,128)(2,1)}, bf16[256,1024]{1,0:T(8,128)(2,1)S(1)}, u32[]{:S(2)}, u32[]{:S(2)}) %collective-permute-start.20) | collective-permute-done | bytes 524320 | tf_op jit(solution)/shard_map/ppermute | solution.py:312
  150.7 0.8 copy-done.6
  151.4 4.2 %shard_map.98 = (bf16[256,1024]{1,0:T(8,128)(2,1)}, bf16[256,1024]{1,0:T(8,128)(2,1)}) custom-call(s32[2]{0:T(128)} %pad_add_fusion.meta, bf16[256,1024]{1,0:T(8,128)(2,1)} %bitcast.18, f32[256,512]{1,0:T(8,128)} %get-tuple-element.30.own_k, f32[256,512]{1,0:T(8,128)} %get-tuple-element.31.own_v, ...), custom_call_target="tpu_custom_call", output_to_operand_aliasing={{0}: (9, {}), {1}: (10, {})} | custom-call | flops 2621440 | bytes 3932160 | tf_op jit(solution)/shard_map/pallas_call | solution.py:235
  (35 shorter events, 0.1 us)
Async XLA Ops:
  2.5 18.0 %collective-permute-start.7 = (bf16[256,1024]{1,0:T(8,128)(2,1)}, bf16[256,1024]{1,0:T(8,128)(2,1)S(1)}, u32[]{:S(2)}, u32[]{:S(2)}) collective-permute-start(bf16[256,1024]{1,0:T(8,128)(2,1)} %shard_map.94), channel_id=1, source_target_pairs={{0,32},{32,64},{64,96},{1,33},{33,65},{65,97},{2,34},{34,66},{66,9... | collective-permute-start | bytes 1572872 | tf_op jit(solution)/shard_map/ppermute | solution.py:288
  6.0 27.1 %collective-permute-start.6 = (bf16[256,1024]{1,0:T(8,128)(2,1)}, bf16[256,1024]{1,0:T(8,128)(2,1)S(1)}, u32[]{:S(2)}, u32[]{:S(2)}) collective-permute-start(bf16[256,1024]{1,0:T(8,128)(2,1)} %shard_map.94), channel_id=1, source_target_pairs={{0,24},{8,32},{32,56},{40,64},{64,88},{72,96},{96,120},{1,25},{9,3... | collective-permute-start | bytes 1572872 | tf_op jit(solution)/shard_map/ppermute | solution.py:288
  9.2 25.9 %collective-permute-start.5 = (bf16[256,1024]{1,0:T(8,128)(2,1)}, bf16[256,1024]{1,0:T(8,128)(2,1)S(1)}, u32[]{:S(2)}, u32[]{:S(2)}) collective-permute-start(bf16[256,1024]{1,0:T(8,128)(2,1)} %shard_map.94), channel_id=1, source_target_pairs={{0,16},{8,24},{16,32},{32,48},{40,56},{48,64},{64,80},{72,88},{80,... | collective-permute-start | bytes 1572872 | tf_op jit(solution)/shard_map/ppermute | solution.py:288
  10.6 32.4 %collective-permute-start.4 = (bf16[256,1024]{1,0:T(8,128)(2,1)}, bf16[256,1024]{1,0:T(8,128)(2,1)S(1)}, u32[]{:S(2)}, u32[]{:S(2)}) collective-permute-start(bf16[256,1024]{1,0:T(8,128)(2,1)} %shard_map.94), channel_id=1, source_target_pairs={{0,8},{8,16},{16,24},{24,32},{32,40},{40,48},{48,56},{56,64},{64,7... | collective-permute-start | bytes 1572872 | tf_op jit(solution)/shard_map/ppermute | solution.py:288
  16.0 51.1 %collective-permute-start.3 = (bf16[256,1024]{1,0:T(8,128)(2,1)}, bf16[256,1024]{1,0:T(8,128)(2,1)S(1)}, u32[]{:S(2)}, u32[]{:S(2)}) collective-permute-start(bf16[256,1024]{1,0:T(8,128)(2,1)} %shard_map.93), channel_id=1, source_target_pairs={{0,32},{32,64},{64,96},{1,33},{33,65},{65,97},{2,34},{34,66},{66,9... | collective-permute-start | bytes 1572872 | tf_op jit(solution)/shard_map/ppermute | solution.py:288
  20.5 22.5 %copy-start.11 = (bf16[256,1024]{1,0:T(8,128)(2,1)}, bf16[256,1024]{1,0:T(8,128)(2,1)S(1)}, u32[]{:S(2)}) copy-start(bf16[256,1024]{1,0:T(8,128)(2,1)S(1)} %collective-permute-done.7.rest_3_) | copy-start | bytes 1572868
  20.5 48.0 %collective-permute-start.2 = (bf16[256,1024]{1,0:T(8,128)(2,1)}, bf16[256,1024]{1,0:T(8,128)(2,1)S(1)}, u32[]{:S(2)}, u32[]{:S(2)}) collective-permute-start(bf16[256,1024]{1,0:T(8,128)(2,1)} %shard_map.93), channel_id=1, source_target_pairs={{0,24},{8,32},{32,56},{40,64},{64,88},{72,96},{96,120},{1,25},{9,3... | collective-permute-start | bytes 1572872 | tf_op jit(solution)/shard_map/ppermute | solution.py:288
  33.1 9.9 %copy-start.12 = (bf16[256,1024]{1,0:T(8,128)(2,1)}, bf16[256,1024]{1,0:T(8,128)(2,1)S(1)}, u32[]{:S(2)}) copy-start(bf16[256,1024]{1,0:T(8,128)(2,1)S(1)} %collective-permute-done.6.rest_2_) | copy-start | bytes 1572868
  33.1 36.9 %collective-permute-start.1 = (bf16[256,1024]{1,0:T(8,128)(2,1)}, bf16[256,1024]{1,0:T(8,128)(2,1)}, u32[]{:S(2)}, u32[]{:S(2)}) collective-permute-start(bf16[256,1024]{1,0:T(8,128)(2,1)} %shard_map.93), channel_id=1, source_target_pairs={{0,16},{8,24},{16,32},{32,48},{40,56},{48,64},{64,80},{72,88},{80,... | collective-permute-start | bytes 1572872 | tf_op jit(solution)/shard_map/ppermute | solution.py:288
  35.2 7.8 %copy-start.13 = (bf16[256,1024]{1,0:T(8,128)(2,1)}, bf16[256,1024]{1,0:T(8,128)(2,1)S(1)}, u32[]{:S(2)}) copy-start(bf16[256,1024]{1,0:T(8,128)(2,1)S(1)} %collective-permute-done.5.rest_1_) | copy-start | bytes 1572868
  35.2 34.8 %collective-permute-start = (bf16[256,1024]{1,0:T(8,128)(2,1)}, bf16[256,1024]{1,0:T(8,128)(2,1)}, u32[]{:S(2)}, u32[]{:S(2)}) collective-permute-start(bf16[256,1024]{1,0:T(8,128)(2,1)} %shard_map.93), channel_id=1, source_target_pairs={{0,8},{8,16},{16,24},{24,32},{32,40},{40,48},{48,56},{56,64},{64,7... | collective-permute-start | bytes 1572872 | tf_op jit(solution)/shard_map/ppermute | solution.py:288
  42.9 0.8 copy-start.14
  65.8 29.2 %collective-permute-start.16 = (bf16[256,1024]{1,0:T(8,128)(2,1)}, bf16[256,1024]{1,0:T(8,128)(2,1)S(1)}, u32[]{:S(2)}, u32[]{:S(2)}) collective-permute-start(bf16[256,1024]{1,0:T(8,128)(2,1)} %get-tuple-element.40), channel_id=1, source_target_pairs={{8,0},{16,8},{24,16},{32,56},{40,32},{48,40},{56,48},{64,88},{72,6... | collective-permute-start | bytes 1572872 | tf_op jit(solution)/shard_map/ppermute | solution.py:300
  67.1 2.8 %copy-start.10 = (bf16[256,1024]{1,0:T(8,128)(2,1)}, bf16[256,1024]{1,0:T(8,128)(2,1)S(1)}, u32[]{:S(2)}) copy-start(bf16[256,1024]{1,0:T(8,128)(2,1)S(1)} %collective-permute-done.3.rest_3_) | copy-start | bytes 1572868
  67.1 29.2 %collective-permute-start.17 = (bf16[256,1024]{1,0:T(8,128)(2,1)}, bf16[256,1024]{1,0:T(8,128)(2,1)S(1)}, u32[]{:S(2)}, u32[]{:S(2)}) collective-permute-start(bf16[256,1024]{1,0:T(8,128)(2,1)} %get-tuple-element.41), channel_id=1, source_target_pairs={{16,0},{24,8},{32,48},{48,32},{56,40},{64,80},{80,64},{88,72},{96,... | collective-permute-start | bytes 1572872 | tf_op jit(solution)/shard_map/ppermute | solution.py:300
  68.5 1.5 copy-start.15
  68.5 27.9 %collective-permute-start.18 = (bf16[256,1024]{1,0:T(8,128)(2,1)}, bf16[256,1024]{1,0:T(8,128)(2,1)S(1)}, u32[]{:S(2)}, u32[]{:S(2)}) collective-permute-start(bf16[256,1024]{1,0:T(8,128)(2,1)} %get-tuple-element.42), channel_id=1, source_target_pairs={{24,0},{32,40},{56,32},{64,72},{88,64},{96,104},{120,96},{25,1},{3... | collective-permute-start | bytes 1572872 | tf_op jit(solution)/shard_map/ppermute | solution.py:300
  70.0 26.4 %copy-start.9 = (bf16[256,1024]{1,0:T(8,128)(2,1)S(1)}, bf16[256,1024]{1,0:T(8,128)(2,1)}, u32[]{:S(2)}) copy-start(bf16[256,1024]{1,0:T(8,128)(2,1)} %get-tuple-element.43) | copy-start | bytes 1572868
  92.2 5.5 %copy-start.16 = (f32[1,128]{1,0:T(1,128)S(1)}, f32[1,128]{1,0:T(1,128)}, u32[]{:S(2)}) copy-start(f32[1,128]{1,0:T(1,128)} %get-tuple-element.36) | copy-start | bytes 1540
  92.2 5.5 %copy-start.17 = (f32[1,128]{1,0:T(1,128)S(1)}, f32[1,128]{1,0:T(1,128)}, u32[]{:S(2)}) copy-start(f32[1,128]{1,0:T(1,128)} %get-tuple-element.37) | copy-start | bytes 1540
  92.2 34.7 %copy-start.7 = (bf16[256,1024]{1,0:T(8,128)(2,1)S(1)}, bf16[256,1024]{1,0:T(8,128)(2,1)}, u32[]{:S(2)}) copy-start(bf16[256,1024]{1,0:T(8,128)(2,1)} %get-tuple-element.35) | copy-start | bytes 1572868
  92.2 34.7 %collective-permute-start.8 = (bf16[256,1024]{1,0:T(8,128)(2,1)}, bf16[256,1024]{1,0:T(8,128)(2,1)S(1)}, u32[]{:S(2)}, u32[]{:S(2)}) collective-permute-start(bf16[256,1024]{1,0:T(8,128)(2,1)} %get-tuple-element.32), channel_id=1, source_target_pairs={{8,0},{16,8},{24,16},{32,56},{40,32},{48,40},{56,48},{64,88},{72,6... | collective-permute-start | bytes 1572872 | tf_op jit(solution)/shard_map/ppermute | solution.py:300
  93.7 33.2 %collective-permute-start.9 = (bf16[256,1024]{1,0:T(8,128)(2,1)}, bf16[256,1024]{1,0:T(8,128)(2,1)S(1)}, u32[]{:S(2)}, u32[]{:S(2)}) collective-permute-start(bf16[256,1024]{1,0:T(8,128)(2,1)} %get-tuple-element.33), channel_id=1, source_target_pairs={{16,0},{24,8},{32,48},{48,32},{56,40},{64,80},{80,64},{88,72},{96,... | collective-permute-start | bytes 1572872 | tf_op jit(solution)/shard_map/ppermute | solution.py:300
  95.0 33.1 %copy-start.3 = (bf16[256,1024]{1,0:T(8,128)(2,1)}, bf16[256,1024]{1,0:T(8,128)(2,1)S(1)}, u32[]{:S(2)}) copy-start(bf16[256,1024]{1,0:T(8,128)(2,1)S(1)} %collective-permute-done.16.rest_0_) | copy-start | bytes 1572868
  95.0 31.9 %collective-permute-start.10 = (bf16[256,1024]{1,0:T(8,128)(2,1)}, bf16[256,1024]{1,0:T(8,128)(2,1)S(1)}, u32[]{:S(2)}, u32[]{:S(2)}) collective-permute-start(bf16[256,1024]{1,0:T(8,128)(2,1)} %get-tuple-element.34), channel_id=1, source_target_pairs={{24,0},{32,40},{56,32},{64,72},{88,64},{96,104},{120,96},{25,1},{3... | collective-permute-start | bytes 1572872 | tf_op jit(solution)/shard_map/ppermute | solution.py:300
  96.3 31.8 %copy-start.4 = (bf16[256,1024]{1,0:T(8,128)(2,1)}, bf16[256,1024]{1,0:T(8,128)(2,1)S(1)}, u32[]{:S(2)}) copy-start(bf16[256,1024]{1,0:T(8,128)(2,1)S(1)} %collective-permute-done.17.rest_1_) | copy-start | bytes 1572868
  96.3 31.7 %copy-start.5 = (bf16[256,1024]{1,0:T(8,128)(2,1)}, bf16[256,1024]{1,0:T(8,128)(2,1)S(1)}, u32[]{:S(2)}) copy-start(bf16[256,1024]{1,0:T(8,128)(2,1)S(1)} %collective-permute-done.18.rest_2_) | copy-start | bytes 1572868
  96.5 31.6 %collective-permute-start.19 = (bf16[256,1024]{1,0:T(8,128)(2,1)S(1)}, bf16[256,1024]{1,0:T(8,128)(2,1)S(1)}, u32[]{:S(2)}, u32[]{:S(2)}) collective-permute-start(bf16[256,1024]{1,0:T(8,128)(2,1)S(1)} %select_select_fusion), channel_id=1, source_target_pairs={{32,0},{40,8},{48,16},{56,24},{64,32},{72,40},{80,48},{88,56},{96,... | collective-permute-start | bytes 1572872 | tf_op jit(solution)/shard_map/ppermute | solution.py:312
  97.8 1.2 collective-permute-start.11
  99.0 3.5 %collective-permute-start.12 = (f32[1,128]{1,0:T(1,128)S(1)}, f32[1,128]{1,0:T(1,128)S(1)}, u32[]{:S(2)}, u32[]{:S(2)}) collective-permute-start(f32[1,128]{1,0:T(1,128)S(1)} %add.30), channel_id=1, source_target_pairs={{0,2},{1,3},{2,0},{3,1},{4,6},{5,7},{6,4},{7,5},{8,10},{9,11},{10,... | collective-permute-start | bytes 1544 | tf_op jit(solution)/shard_map/ppermute | solution.py:273
  102.5 5.0 %collective-permute-start.13 = (f32[1,128]{1,0:T(1,128)S(1)}, f32[1,128]{1,0:T(1,128)S(1)}, u32[]{:S(2)}, u32[]{:S(2)}) collective-permute-start(f32[1,128]{1,0:T(1,128)S(1)} %add.31), channel_id=1, source_target_pairs={{0,4},{1,5},{2,6},{3,7},{4,0},{5,1},{6,2},{7,3},{8,12},{9,13},{10,... | collective-permute-start | bytes 1544 | tf_op jit(solution)/shard_map/ppermute | solution.py:273
  107.6 13.7 %collective-permute-start.14 = (f32[1,128]{1,0:T(1,128)S(1)}, f32[1,128]{1,0:T(1,128)S(1)}, u32[]{:S(2)}, u32[]{:S(2)}) collective-permute-start(f32[1,128]{1,0:T(1,128)S(1)} %add.32), channel_id=1, source_target_pairs={{0,32},{8,40},{16,48},{24,56},{32,0},{40,8},{48,16},{56,24},{64,96... | collective-permute-start | bytes 1544 | tf_op jit(solution)/shard_map/ppermute | solution.py:273
  121.3 5.6 %collective-permute-start.15 = (f32[1,128]{1,0:T(1,128)S(1)}, f32[1,128]{1,0:T(1,128)S(1)}, u32[]{:S(2)}, u32[]{:S(2)}) collective-permute-start(f32[1,128]{1,0:T(1,128)S(1)} %add.33), channel_id=1, source_target_pairs={{0,64},{8,72},{16,80},{24,88},{32,96},{40,104},{48,112},{56,120},{... | collective-permute-start | bytes 1544 | tf_op jit(solution)/shard_map/ppermute | solution.py:273
  126.9 6.1 %copy-start = (bf16[256,1024]{1,0:T(8,128)(2,1)}, bf16[256,1024]{1,0:T(8,128)(2,1)S(1)}, u32[]{:S(2)}) copy-start(bf16[256,1024]{1,0:T(8,128)(2,1)S(1)} %collective-permute-done.8.rest_0_) | copy-start | bytes 1572868
  126.9 6.1 %copy-start.1 = (bf16[256,1024]{1,0:T(8,128)(2,1)}, bf16[256,1024]{1,0:T(8,128)(2,1)S(1)}, u32[]{:S(2)}) copy-start(bf16[256,1024]{1,0:T(8,128)(2,1)S(1)} %collective-permute-done.9.rest_1_) | copy-start | bytes 1572868
  126.9 6.1 %copy-start.2 = (bf16[256,1024]{1,0:T(8,128)(2,1)}, bf16[256,1024]{1,0:T(8,128)(2,1)S(1)}, u32[]{:S(2)}) copy-start(bf16[256,1024]{1,0:T(8,128)(2,1)S(1)} %collective-permute-done.10.rest_2_) | copy-start | bytes 1572868
  128.1 0.8 copy-start.8
  133.1 17.6 %collective-permute-start.20 = (bf16[256,1024]{1,0:T(8,128)(2,1)}, bf16[256,1024]{1,0:T(8,128)(2,1)S(1)}, u32[]{:S(2)}, u32[]{:S(2)}) collective-permute-start(bf16[256,1024]{1,0:T(8,128)(2,1)} %select_select_fusion.1), channel_id=1, source_target_pairs={{32,0},{40,8},{48,16},{56,24},{64,32},{72,40},{80,48},{88,56},{96,... | collective-permute-start | bytes 1572872 | tf_op jit(solution)/shard_map/ppermute | solution.py:312
  134.4 3.6 %collective-permute-start.21 = (f32[1,128]{1,0:T(1,128)S(1)}, f32[1,128]{1,0:T(1,128)S(1)}, u32[]{:S(2)}, u32[]{:S(2)}) collective-permute-start(f32[1,128]{1,0:T(1,128)S(1)} %add.34), channel_id=1, source_target_pairs={{0,8},{8,0},{16,24},{24,16},{32,40},{40,32},{48,56},{56,48},{64,72... | collective-permute-start | bytes 1544 | tf_op jit(solution)/shard_map/ppermute | solution.py:273
  138.0 5.0 %collective-permute-start.22 = (f32[1,128]{1,0:T(1,128)S(1)}, f32[1,128]{1,0:T(1,128)S(1)}, u32[]{:S(2)}, u32[]{:S(2)}) collective-permute-start(f32[1,128]{1,0:T(1,128)S(1)} %add.35), channel_id=1, source_target_pairs={{0,16},{8,24},{16,0},{24,8},{32,48},{40,56},{48,32},{56,40},{64,80... | collective-permute-start | bytes 1544 | tf_op jit(solution)/shard_map/ppermute | solution.py:273
  150.7 0.8 copy-start.6

commit v3 on v2

--- a/solution.py
+++ b/solution.py
@@ -11,6 +11,7 @@
 SPAN = DOC_IMG + 1
 HEADS = (4, 4)
 HD = 128
+PER = 2
 MASKED = -1e30
 SCALE = HD**-0.5
 LOG2E = 1.4426950408889634
@@ -52,61 +53,102 @@
 
 
 def head_work(
-    images, meta, q_ref, do_ref, key_ref, value_ref, recv, gain_ref,
-    dq_ref, own_k, own_v, parts, gain_part, s_ref, dp_ref, normed, dk_ref, dv_ref,
+    first, meta, q_ref, do_ref, key_ref, value_ref, recv, gain_ref,
+    dq_ref, own_k, own_v, parts, gain_part, s_ref, dp_ref, normed, both_keys, both_values, dk_ref, dv_ref,
 ):
     shard, position = meta[0], meta[1]
     gain = gain_ref[...]
     tokens = q_ref.shape[0]
     group = q_ref.shape[1] // HD
-    token = lax.broadcasted_iota(jnp.int32, (1, 2 * tokens), 1) % tokens
+    cols = PER * tokens
+    token = lax.broadcasted_iota(jnp.int32, (1, cols), 1) % tokens
+    images = tuple(range(SPAN if first else DOC_IMG))
+    blocks = images[1:] if first else images
     bias = {}
     for i in images:
         raw = key_ref[...] if i == 0 else recv[i - 1][:, :HD]
-        normed[i] = (unit_norm(raw)[0] * gain).astype(jnp.bfloat16)
-        if i == 0:
+        keys = (unit_norm(raw)[0] * gain).astype(jnp.bfloat16)
+        if first and i in (0, DOC_IMG):
+            half = slice(HD, 2 * HD) if i == 0 else slice(0, HD)
+            both_keys[:, half] = keys
+            both_values[:, half] = value_ref[...] if i == 0 else recv[i - 1][:, HD:]
+        else:
+            normed[i] = keys
+        if first:
+            bias[i] = jnp.where(token < position, 0.0, MASKED)
+        elif i == 0:
             bias[i] = jnp.where(token >= position, 0.0, MASKED)
-        elif len(images) == SPAN:
-            bias[i] = jnp.where(token < position, 0.0, MASKED)
         else:
             bias[i] = jnp.where(i <= shard, 0.0, MASKED)
-    for pair in range(group // 2):
-        heads = [2 * pair, 2 * pair + 1]
-        q_pair = jnp.concatenate([q_ref[:, g * HD : (g + 1) * HD] for g in heads], 0)
-        do_pair = jnp.concatenate([do_ref[:, g * HD : (g + 1) * HD] for g in heads], 0)
+    if first:
+        row = lax.broadcasted_iota(jnp.int32, (cols, HD), 0) % tokens
+        early = jnp.where(row < position, 1.0, 0.0).astype(jnp.bfloat16)
+        late = jnp.where(row >= position, 1.0, 0.0).astype(jnp.bfloat16)
+    def load(step):
+        heads = [PER * step + j for j in range(PER)]
+        q_rows = jnp.concatenate([q_ref[:, g * HD : (g + 1) * HD] for g in heads], 0)
+        do_rows = jnp.concatenate([do_ref[:, g * HD : (g + 1) * HD] for g in heads], 0)
+        if first:
+            q_both = jnp.concatenate([q_rows * early, q_rows * late], 1)
+            do_both = jnp.concatenate([do_rows * early, do_rows * late], 1)
+        return heads, q_rows, do_rows, q_both if first else None, do_both if first else None
+
+    def scored(step, q_rows, q_both):
         top = None
-        for i in images:
-            scores = dot(normed[i], q_pair, NT) * (SCALE * LOG2E) + bias[i]
-            s_ref[i] = scores
+        for i in blocks:
+            if first and i == DOC_IMG:
+                scores = dot(both_keys[...], q_both, NT) * (SCALE * LOG2E)
+            else:
+                scores = dot(normed[i], q_rows, NT) * (SCALE * LOG2E) + bias[i]
+            s_ref[step % 2, i] = scores
             high = jnp.max(scores, 0, keepdims=True)
             top = high if top is None else jnp.maximum(top, high)
+        return top
+
+    steps = group // PER
+    at_hand = load(0)
+    top = scored(0, at_hand[1], at_hand[3])
+    for step in range(steps):
+        heads, q_rows, do_rows, q_both, do_both = at_hand
         total = 0.0
         weighted = 0.0
-        for i in images:
-            value = value_ref[...] if i == 0 else recv[i - 1][:, HD:]
-            dprob = dot(value, do_pair, NT)
-            weight = jnp.exp2(s_ref[i] - top)
-            s_ref[i] = weight
-            dp_ref[i] = dprob
+        for i in blocks:
+            if first and i == DOC_IMG:
+                dprob = dot(both_values[...], do_both, NT)
+            else:
+                dprob = dot(value_ref[...] if i == 0 else recv[i - 1][:, HD:], do_rows, NT)
+            weight = jnp.exp2(s_ref[step % 2, i] - top)
+            s_ref[step % 2, i] = weight
+            dp_ref[step % 2, i] = dprob
             total = total + jnp.sum(weight, 0, keepdims=True)
             weighted = weighted + jnp.sum(weight * dprob, 0, keepdims=True)
         inverse = 1.0 / total
         delta = weighted * inverse
-        dq_turned = 0.0
-        for i in images:
-            prob = s_ref[i] * inverse
+        if step + 1 < steps:
+            at_hand = load(step + 1)
+            top = scored(step + 1, at_hand[1], at_hand[3])
+        dq = 0.0
+        for i in blocks:
+            prob = s_ref[step % 2, i] * inverse
             prob_low = prob.astype(jnp.bfloat16)
-            dscore = (prob * (dp_ref[i] - delta)).astype(jnp.bfloat16)
-            dv = dot(prob_low, do_pair, NN)
-            dk = dot(dscore, q_pair, NN)
-            if pair == 0:
-                dv_ref[i] = dv
-                dk_ref[i] = dk
+            dscore = (prob * (dp_ref[step % 2, i] - delta)).astype(jnp.bfloat16)
+            if first and i == DOC_IMG:
+                dv = dot(prob_low, do_both, NN)
+                dk = dot(dscore, q_both, NN)
+                pieces = ((i, dk[:, :HD], dv[:, :HD]), (0, dk[:, HD:], dv[:, HD:]))
+                dq_both = dot(both_keys[...], dscore, TN)
+                dq = dq + jnp.where(token < position, dq_both[:HD], dq_both[HD:])
             else:
-                dv_ref[i] += dv
-                dk_ref[i] += dk
-            dq_turned = dq_turned + dot(normed[i], dscore, TN)
-        dq = (dq_turned.T * SCALE).astype(jnp.bfloat16)
+                pieces = ((i, dot(dscore, q_rows, NN), dot(prob_low, do_rows, NN)),)
+                dq = dq + dot(normed[i], dscore, TN)
+            for image, dk, dv in pieces:
+                if step == 0:
+                    dk_ref[image] = dk
+                    dv_ref[image] = dv
+                else:
+                    dk_ref[image] += dk
+                    dv_ref[image] += dv
+        dq = (dq.T * SCALE).astype(jnp.bfloat16)
         for j, g in enumerate(heads):
             dq_ref[:, g * HD : (g + 1) * HD] = dq[j * tokens : (j + 1) * tokens]
     gain_sum = jnp.zeros_like(gain)
@@ -141,11 +183,11 @@
 
     @pl.when(meta[0] == 0)
     def _():
-        head_work(tuple(range(SPAN)), *args)
+        head_work(True, *args)
 
     @pl.when(meta[0] != 0)
     def _():
-        head_work(tuple(range(DOC_IMG)), *args)
+        head_work(False, *args)
 
 
 def attend(meta, queries, grad_out, key_raw, values, recv, gain, dq, chunk):
@@ -178,9 +220,11 @@
         + [jax.ShapeDtypeStruct((rows, 2 * heads * HD), bf16)] * DOC_IMG
         + [jax.ShapeDtypeStruct((1, HD), f32)],
         scratch_shapes=[
-            pltpu.VMEM((SPAN, rows, 2 * tokens), f32),
-            pltpu.VMEM((SPAN, rows, 2 * tokens), f32),
+            pltpu.VMEM((2, SPAN, rows, PER * tokens), f32),
+            pltpu.VMEM((2, SPAN, rows, PER * tokens), f32),
             pltpu.VMEM((SPAN, rows, HD), bf16),
+            pltpu.VMEM((rows, 2 * HD), bf16),
+            pltpu.VMEM((rows, 2 * HD), bf16),
             pltpu.VMEM((SPAN, rows, HD), f32),
             pltpu.VMEM((SPAN, rows, HD), f32),
         ],
@@ -201,29 +245,32 @@
         rest = rest[2:]
     gk_ref, gv_ref = rest
     shard = meta[0]
-    unit, inv_rms = unit_norm(key_ref[...])
-    dk, dv = own_k[...], own_v[...]
-    for distance, ref in enumerate(back, 1):
-        dk_part = ref[:, :HD].astype(jnp.float32)
-        dv_part = ref[:, HD:].astype(jnp.float32)
-        if distance < DOC_IMG:
-            held = shard + distance < DOC_IMG
-            dk_part = jnp.where(held, dk_part, 0.0)
-            dv_part = jnp.where(held, dv_part, 0.0)
-        dk = dk + dk_part
-        dv = dv + dv_part
-    scaled = dk * gain_ref[...]
-    inner = jnp.mean(scaled * unit, -1, keepdims=True)
-    gk_ref[...] = (inv_rms * (scaled - unit * inner)).astype(gk_ref.dtype)
-    gv_ref[...] = dv.astype(gv_ref.dtype)
+    for head in range(key_ref.shape[1] // HD):
+        at = slice(head * HD, (head + 1) * HD)
+        left = 2 * HD * head
+        unit, inv_rms = unit_norm(key_ref[:, at])
+        dk, dv = own_k[:, at], own_v[:, at]
+        for distance, ref in enumerate(back, 1):
+            dk_part = ref[:, left : left + HD].astype(jnp.float32)
+            dv_part = ref[:, left + HD : left + 2 * HD].astype(jnp.float32)
+            if distance < DOC_IMG:
+                held = shard + distance < DOC_IMG
+                dk_part = jnp.where(held, dk_part, 0.0)
+                dv_part = jnp.where(held, dv_part, 0.0)
+            dk = dk + dk_part
+            dv = dv + dv_part
+        scaled = dk * gain_ref[...]
+        inner = jnp.mean(scaled * unit, -1, keepdims=True)
+        gk_ref[:, at] = (inv_rms * (scaled - unit * inner)).astype(gk_ref.dtype)
+        gv_ref[:, at] = dv.astype(gv_ref.dtype)
 
 
 def finish(meta, key_raw, own_k, own_v, back, gain, done, chunk):
     rows, width = key_raw.shape
     first, heads = sum(HEADS[:chunk]), HEADS[chunk]
-    local = pl.BlockSpec((rows, HD), lambda h: (0, h))
-    part = pl.BlockSpec((rows, 2 * HD), lambda h: (0, h))
-    placed = pl.BlockSpec((rows, HD), lambda h: (0, first + h))
+    local = pl.BlockSpec((rows, 2 * HD), lambda h: (0, h))
+    part = pl.BlockSpec((rows, 4 * HD), lambda h: (0, h))
+    placed = pl.BlockSpec((rows, 2 * HD), lambda h: (0, first // 2 + h))
     args = [meta, key_raw, own_k, own_v, *back, gain]
     in_specs = [pl.BlockSpec(memory_space=pltpu.SMEM), placed, local, local]
     in_specs += [part] * DOC_IMG + [pl.BlockSpec((1, HD), lambda h: (0, 0))]
@@ -234,7 +281,7 @@
         args += done
     return pl.pallas_call(
         functools.partial(finish_kernel, aliased=done is not None),
-        grid=(heads,),
+        grid=(heads // 2,),
         in_specs=in_specs,
         out_specs=[placed, placed],
         out_shape=[jax.ShapeDtypeStruct(key_raw.shape, jnp.bfloat16)] * 2,

time: 157 us -> 150 us (0.955)
  Pallas kernels: 56.4 us -> 46.1 us
  starting transfers between devices: 61.2 us -> 64 us
    pallas_call x2, Pallas kernels: 44.3 us -> 36.5 us  [attend(): pl.pallas_call(functools.partial(attend_kernel, aliased=dq is not None),...]
    ppermute x7, starting transfers between devices: 23.4 us -> 26.2 us  [all_sum(): value = value + lax.ppermute(value, axis, pairs)]
    pallas_call x2, Pallas kernels: 8.34 us -> 5.85 us  [finish(): pl.pallas_call(functools.partial(finish_kernel, aliased=done is not None)...]
  transfers between devices with their start and end apart: 23 -> 23, of which waited for: 9 -> 10; matrix products, arithmetic and copies ran while one was open for 2% -> 2% of each run, Pallas kernels for 30% -> 26%
where the time goes in v3:
time: 150 us; the launch traced here: 149 us
  starting transfers between devices  64 us (43%)
  Pallas kernels  46.1 us (31%)
  waiting for transfers between devices  32.7 us (22%)
  local copies, waits for them, and re-layouts  2.43 us (2%)
  other arithmetic  2.39 us (2%)
  between operations  1.68 us (1%)
    pallas_call x2, Pallas kernels, attend(): pl.pallas_call(functools.partial(attend_kernel, aliased=dq is not None),...  36.5 us
    ppermute x8, starting transfers between devices, shards(): recv.append([lax.ppermute(packed, 'ctx', to) for to in pairs])  27.2 us
    ppermute x7, starting transfers between devices, all_sum(): value = value + lax.ppermute(value, axis, pairs)  26.2 us
    ppermute x7, waiting for transfers between devices, all_sum(): value = value + lax.ppermute(value, axis, pairs)  13.8 us
    ppermute x8, waiting for transfers between devices, shards(): recv.append([lax.ppermute(packed, 'ctx', to) for to in pairs])  10 us
    ppermute x2, waiting for transfers between devices, shards(): back[chunk].append(lax.ppermute(handed, 'ctx', before_pairs(count)))  8.18 us
    ppermute x6, starting transfers between devices, shards(): lax.ppermute(parts[distance - 1], 'ctx', ring_pairs(count, distance))  8.06 us
    pallas_call x2, Pallas kernels, finish(): pl.pallas_call(functools.partial(finish_kernel, aliased=done is not None)...  5.85 us
  transfers between devices with their start and end apart: 23, of which 10 were waited for; matrix products, arithmetic and copies ran while one was open for 2% of the time, Pallas kernels for 26%

profile of v3, /device:TPU:0, one launch (start us, length us, event | category | flops | bytes accessed | tf_op | source)
XLA Modules:
  0.0 149.4 jit_solution(5867158902148831586)
XLA Ops:
  0.6 1.9 %shard_map.94 = bf16[256,1024]{1,0:T(8,128)(2,1)} custom-call(bf16[256,1024]{1,0:T(8,128)(2,1)} %bitcast.13, bf16[256,1024]{1,0:T(8,128)(2,1)} %bitcast.19), custom_call_target="tpu_custom_call" | custom-call | bytes 1048576 | tf_op jit(solution)/shard_map/pallas_call | solution.py:45
  2.5 3.5 %collective-permute-start.7 = (bf16[256,1024]{1,0:T(8,128)(2,1)}, bf16[256,1024]{1,0:T(8,128)(2,1)S(1)}, u32[]{:S(2)}, u32[]{:S(2)}) collective-permute-start(bf16[256,1024]{1,0:T(8,128)(2,1)} %shard_map.94), channel_id=1, source_target_pairs={{0,32},{32,64},{64,96},{1,33},{33,65},{65,97},{2,34},{34,66},{66,9... | collective-permute-start | bytes 1572872 | tf_op jit(solution)/shard_map/ppermute | solution.py:335
  6.0 3.2 %collective-permute-start.6 = (bf16[256,1024]{1,0:T(8,128)(2,1)}, bf16[256,1024]{1,0:T(8,128)(2,1)S(1)}, u32[]{:S(2)}, u32[]{:S(2)}) collective-permute-start(bf16[256,1024]{1,0:T(8,128)(2,1)} %shard_map.94), channel_id=1, source_target_pairs={{0,24},{8,32},{32,56},{40,64},{64,88},{72,96},{96,120},{1,25},{9,3... | collective-permute-start | bytes 1572872 | tf_op jit(solution)/shard_map/ppermute | solution.py:335
  9.2 1.3 collective-permute-start.5
  10.6 3.6 %collective-permute-start.4 = (bf16[256,1024]{1,0:T(8,128)(2,1)}, bf16[256,1024]{1,0:T(8,128)(2,1)S(1)}, u32[]{:S(2)}, u32[]{:S(2)}) collective-permute-start(bf16[256,1024]{1,0:T(8,128)(2,1)} %shard_map.94), channel_id=1, source_target_pairs={{0,8},{8,16},{16,24},{24,32},{32,40},{40,48},{48,56},{56,64},{64,7... | collective-permute-start | bytes 1572872 | tf_op jit(solution)/shard_map/ppermute | solution.py:335
  14.1 1.9 %shard_map.93 = bf16[256,1024]{1,0:T(8,128)(2,1)} custom-call(bf16[256,1024]{1,0:T(8,128)(2,1)} %bitcast.14, bf16[256,1024]{1,0:T(8,128)(2,1)} %bitcast.20), custom_call_target="tpu_custom_call" | custom-call | bytes 1048576 | tf_op jit(solution)/shard_map/pallas_call | solution.py:45
  16.0 3.1 %collective-permute-start.3 = (bf16[256,1024]{1,0:T(8,128)(2,1)}, bf16[256,1024]{1,0:T(8,128)(2,1)S(1)}, u32[]{:S(2)}, u32[]{:S(2)}) collective-permute-start(bf16[256,1024]{1,0:T(8,128)(2,1)} %shard_map.93), channel_id=1, source_target_pairs={{0,32},{32,64},{64,96},{1,33},{33,65},{65,97},{2,34},{34,66},{66,9... | collective-permute-start | bytes 1572872 | tf_op jit(solution)/shard_map/ppermute | solution.py:335
  19.8 0.7 pad_add_fusion.meta
  20.5 0.0 collective-permute-done.7.rest_3_
  20.5 2.6 %collective-permute-start.2 = (bf16[256,1024]{1,0:T(8,128)(2,1)}, bf16[256,1024]{1,0:T(8,128)(2,1)S(1)}, u32[]{:S(2)}, u32[]{:S(2)}) collective-permute-start(bf16[256,1024]{1,0:T(8,128)(2,1)} %shard_map.93), channel_id=1, source_target_pairs={{0,24},{8,32},{32,56},{40,64},{64,88},{72,96},{96,120},{1,25},{9,3... | collective-permute-start | bytes 1572872 | tf_op jit(solution)/shard_map/ppermute | solution.py:335
  23.1 10.0 %collective-permute-done.6.rest_2_ = bf16[256,1024]{1,0:T(8,128)(2,1)S(1)} collective-permute-done((bf16[256,1024]{1,0:T(8,128)(2,1)}, bf16[256,1024]{1,0:T(8,128)(2,1)S(1)}, u32[]{:S(2)}, u32[]{:S(2)}) %collective-permute-start.6) | collective-permute-done | bytes 524320 | tf_op jit(solution)/shard_map/ppermute | solution.py:335
  33.1 2.1 %collective-permute-start.1 = (bf16[256,1024]{1,0:T(8,128)(2,1)}, bf16[256,1024]{1,0:T(8,128)(2,1)}, u32[]{:S(2)}, u32[]{:S(2)}) collective-permute-start(bf16[256,1024]{1,0:T(8,128)(2,1)} %shard_map.93), channel_id=1, source_target_pairs={{0,16},{8,24},{16,32},{32,48},{40,56},{48,64},{64,80},{72,88},{80,... | collective-permute-start | bytes 1572872 | tf_op jit(solution)/shard_map/ppermute | solution.py:335
  35.2 0.0 collective-permute-done.5.rest_1_
  35.2 7.8 %collective-permute-start = (bf16[256,1024]{1,0:T(8,128)(2,1)}, bf16[256,1024]{1,0:T(8,128)(2,1)}, u32[]{:S(2)}, u32[]{:S(2)}) collective-permute-start(bf16[256,1024]{1,0:T(8,128)(2,1)} %shard_map.93), channel_id=1, source_target_pairs={{0,8},{8,16},{16,24},{24,32},{32,40},{40,48},{48,56},{56,64},{64,7... | collective-permute-start | bytes 1572872 | tf_op jit(solution)/shard_map/ppermute | solution.py:335
  42.9 0.0 collective-permute-done.4.rest_0_
  42.9 0.0 copy-done.12
  43.0 0.8 copy-done.14
  43.7 18.2 %shard_map.95 = (bf16[128,8192]{1,0:T(8,128)(2,1)}, f32[256,512]{1,0:T(8,128)}, f32[256,512]{1,0:T(8,128)}, bf16[256,1024]{1,0:T(8,128)(2,1)}, bf16[256,1024]{1,...) custom-call(s32[2]{0:T(128)} %pad_add_fusion.meta, ...), custom_call_target="tpu_custom_call" | custom-call | flops 6710886400 | bytes 18874368 | tf_op jit(solution)/shard_map/pallas_call | solution.py:213
  61.9 1.3 collective-permute-start.16
  63.2 0.0 collective-permute-done.3.rest_3_
  63.2 1.3 collective-permute-start.17
  64.5 0.0 collective-permute-done.2.rest_2_
  64.6 0.0 copy-start.15
  64.6 1.5 collective-permute-start.18
  66.0 0.0 collective-permute-done.1.rest_1_
  66.1 0.0 collective-permute-done.rest_0_
  66.1 18.3 %shard_map.96 = (bf16[128,8192]{1,0:T(8,128)(2,1)}, f32[256,512]{1,0:T(8,128)}, f32[256,512]{1,0:T(8,128)}, bf16[256,1024]{1,0:T(8,128)(2,1)}, bf16[256,1024]{1,...) custom-call(s32[2]{0:T(128)} %pad_add_fusion.meta, ...), custom_call_target="tpu_custom_call", output_to_operand_aliasing={{0}: (10, {})} | custom-call | flops 6710886400 | bytes 18874368 | tf_op jit(solution)/shard_map/pallas_call | solution.py:213
  84.4 0.0 copy-start.16
  84.5 1.4 collective-permute-start.8
  85.9 1.3 collective-permute-start.9
  87.2 0.0 collective-permute-done.16.rest_0_
  87.2 1.3 collective-permute-start.10
  88.5 0.0 collective-permute-done.17.rest_1_
  88.5 0.0 copy-start.4
  88.5 0.6 collective-permute-done.18.rest_2_
  89.2 0.1 select_select_fusion
  89.3 1.3 collective-permute-start.19
  90.6 0.1 collective-permute-start.11
  90.7 1.1 collective-permute-done.11
  91.8 1.6 %collective-permute-start.12 = (f32[1,128]{1,0:T(1,128)S(1)}, f32[1,128]{1,0:T(1,128)S(1)}, u32[]{:S(2)}, u32[]{:S(2)}) collective-permute-start(f32[1,128]{1,0:T(1,128)S(1)} %add.30), channel_id=1, source_target_pairs={{0,2},{1,3},{2,0},{3,1},{4,6},{5,7},{6,4},{7,5},{8,10},{9,11},{10,... | collective-permute-start | bytes 1544 | tf_op jit(solution)/shard_map/ppermute | solution.py:320
  93.4 2.0 %collective-permute-done.12 = f32[1,128]{1,0:T(1,128)S(1)} collective-permute-done((f32[1,128]{1,0:T(1,128)S(1)}, f32[1,128]{1,0:T(1,128)S(1)}, u32[]{:S(2)}, u32[]{:S(2)}) %collective-permute-start.12) | collective-permute-done | bytes 544 | tf_op jit(solution)/shard_map/ppermute | solution.py:320
  95.4 3.2 %collective-permute-start.13 = (f32[1,128]{1,0:T(1,128)S(1)}, f32[1,128]{1,0:T(1,128)S(1)}, u32[]{:S(2)}, u32[]{:S(2)}) collective-permute-start(f32[1,128]{1,0:T(1,128)S(1)} %add.31), channel_id=1, source_target_pairs={{0,4},{1,5},{2,6},{3,7},{4,0},{5,1},{6,2},{7,3},{8,12},{9,13},{10,... | collective-permute-start | bytes 1544 | tf_op jit(solution)/shard_map/ppermute | solution.py:320
  98.6 1.8 %collective-permute-done.13 = f32[1,128]{1,0:T(1,128)S(1)} collective-permute-done((f32[1,128]{1,0:T(1,128)S(1)}, f32[1,128]{1,0:T(1,128)S(1)}, u32[]{:S(2)}, u32[]{:S(2)}) %collective-permute-start.13) | collective-permute-done | bytes 544 | tf_op jit(solution)/shard_map/ppermute | solution.py:320
  100.4 14.5 %collective-permute-start.14 = (f32[1,128]{1,0:T(1,128)S(1)}, f32[1,128]{1,0:T(1,128)S(1)}, u32[]{:S(2)}, u32[]{:S(2)}) collective-permute-start(f32[1,128]{1,0:T(1,128)S(1)} %add.32), channel_id=1, source_target_pairs={{0,32},{8,40},{16,48},{24,56},{32,0},{40,8},{48,16},{56,24},{64,96... | collective-permute-start | bytes 1544 | tf_op jit(solution)/shard_map/ppermute | solution.py:320
  114.9 1.5 %collective-permute-done.14 = f32[1,128]{1,0:T(1,128)S(1)} collective-permute-done((f32[1,128]{1,0:T(1,128)S(1)}, f32[1,128]{1,0:T(1,128)S(1)}, u32[]{:S(2)}, u32[]{:S(2)}) %collective-permute-start.14) | collective-permute-done | bytes 544 | tf_op jit(solution)/shard_map/ppermute | solution.py:320
  116.4 4.1 %collective-permute-start.15 = (f32[1,128]{1,0:T(1,128)S(1)}, f32[1,128]{1,0:T(1,128)S(1)}, u32[]{:S(2)}, u32[]{:S(2)}) collective-permute-start(f32[1,128]{1,0:T(1,128)S(1)} %add.33), channel_id=1, source_target_pairs={{0,64},{8,72},{16,80},{24,88},{32,96},{40,104},{48,112},{56,120},{... | collective-permute-start | bytes 1544 | tf_op jit(solution)/shard_map/ppermute | solution.py:320
  120.5 1.5 %collective-permute-done.15 = f32[1,128]{1,0:T(1,128)S(1)} collective-permute-done((f32[1,128]{1,0:T(1,128)S(1)}, f32[1,128]{1,0:T(1,128)S(1)}, u32[]{:S(2)}, u32[]{:S(2)}) %collective-permute-start.15) | collective-permute-done | bytes 544 | tf_op jit(solution)/shard_map/ppermute | solution.py:320
  122.0 0.0 collective-permute-done.8.rest_0_
  122.0 0.0 collective-permute-done.9.rest_1_
  122.1 0.0 collective-permute-done.10.rest_2_
  122.1 1.1 select_select_fusion.1
  123.2 0.0 copy-done.3
  123.2 0.0 collective-permute-done.19.rest_3_
  123.2 0.8 copy-done.8
  124.0 2.9 %shard_map.97 = (bf16[256,1024]{1,0:T(8,128)(2,1)}, bf16[256,1024]{1,0:T(8,128)(2,1)}) custom-call(s32[2]{0:T(128)} %pad_add_fusion.meta, bf16[256,1024]{1,0:T(8,128)(2,1)} %bitcast.17, f32[256,512]{1,0:T(8,128)} %get-tuple-element.38.own_k, f32[256,512]{1,0:T(8,128)} %get-tuple-element.39.own_v, bf16[256,1024]{1,0:T(8,128)(2,1)} %copy-done.3, ...), custom_call_target="tpu_custom_call" | custom-call | flops 2621440 | bytes 3932160 | tf_op jit(solution)/shard_map/pallas_call | solution.py:282
  127.0 1.3 collective-permute-start.20
  128.3 0.1 collective-permute-start.21
  128.4 3.5 %collective-permute-done.21 = f32[1,128]{1,0:T(1,128)S(1)} collective-permute-done((f32[1,128]{1,0:T(1,128)S(1)}, f32[1,128]{1,0:T(1,128)S(1)}, u32[]{:S(2)}, u32[]{:S(2)}) %collective-permute-start.21) | collective-permute-done | bytes 544 | tf_op jit(solution)/shard_map/ppermute | solution.py:320
  131.9 2.7 %collective-permute-start.22 = (f32[1,128]{1,0:T(1,128)S(1)}, f32[1,128]{1,0:T(1,128)S(1)}, u32[]{:S(2)}, u32[]{:S(2)}) collective-permute-start(f32[1,128]{1,0:T(1,128)S(1)} %add.35), channel_id=1, source_target_pairs={{0,16},{8,24},{16,0},{24,8},{32,48},{40,56},{48,32},{56,40},{64,80... | collective-permute-start | bytes 1544 | tf_op jit(solution)/shard_map/ppermute | solution.py:320
  134.6 2.3 %collective-permute-done.22 = f32[1,128]{1,0:T(1,128)S(1)} collective-permute-done((f32[1,128]{1,0:T(1,128)S(1)}, f32[1,128]{1,0:T(1,128)S(1)}, u32[]{:S(2)}, u32[]{:S(2)}) %collective-permute-start.22) | collective-permute-done | bytes 544 | tf_op jit(solution)/shard_map/ppermute | solution.py:320
  136.9 0.5 add_bitcast_fusion
  137.4 8.2 %collective-permute-done.20.rest_3_ = bf16[256,1024]{1,0:T(8,128)(2,1)S(1)} collective-permute-done((bf16[256,1024]{1,0:T(8,128)(2,1)}, bf16[256,1024]{1,0:T(8,128)(2,1)S(1)}, u32[]{:S(2)}, u32[]{:S(2)}) %collective-permute-start.20) | collective-permute-done | bytes 524320 | tf_op jit(solution)/shard_map/ppermute | solution.py:359
  145.6 0.8 copy-done.6
  146.4 2.9 %shard_map.98 = (bf16[256,1024]{1,0:T(8,128)(2,1)}, bf16[256,1024]{1,0:T(8,128)(2,1)}) custom-call(s32[2]{0:T(128)} %pad_add_fusion.meta, bf16[256,1024]{1,0:T(8,128)(2,1)} %bitcast.18, f32[256,512]{1,0:T(8,128)} %get-tuple-element.30.own_k, f32[256,512]{1,0:T(8,128)} %get-tuple-element.31.own_v, ...), custom_call_target="tpu_custom_call", output_to_operand_aliasing={{0}: (9, {}), {1}: (10, {})} | custom-call | flops 2621440 | bytes 3932160 | tf_op jit(solution)/shard_map/pallas_call | solution.py:282
  (35 shorter events, 0.1 us)
Async XLA Ops:
  2.5 18.0 %collective-permute-start.7 = (bf16[256,1024]{1,0:T(8,128)(2,1)}, bf16[256,1024]{1,0:T(8,128)(2,1)S(1)}, u32[]{:S(2)}, u32[]{:S(2)}) collective-permute-start(bf16[256,1024]{1,0:T(8,128)(2,1)} %shard_map.94), channel_id=1, source_target_pairs={{0,32},{32,64},{64,96},{1,33},{33,65},{65,97},{2,34},{34,66},{66,9... | collective-permute-start | bytes 1572872 | tf_op jit(solution)/shard_map/ppermute | solution.py:335
  6.0 27.1 %collective-permute-start.6 = (bf16[256,1024]{1,0:T(8,128)(2,1)}, bf16[256,1024]{1,0:T(8,128)(2,1)S(1)}, u32[]{:S(2)}, u32[]{:S(2)}) collective-permute-start(bf16[256,1024]{1,0:T(8,128)(2,1)} %shard_map.94), channel_id=1, source_target_pairs={{0,24},{8,32},{32,56},{40,64},{64,88},{72,96},{96,120},{1,25},{9,3... | collective-permute-start | bytes 1572872 | tf_op jit(solution)/shard_map/ppermute | solution.py:335
  9.2 25.9 %collective-permute-start.5 = (bf16[256,1024]{1,0:T(8,128)(2,1)}, bf16[256,1024]{1,0:T(8,128)(2,1)S(1)}, u32[]{:S(2)}, u32[]{:S(2)}) collective-permute-start(bf16[256,1024]{1,0:T(8,128)(2,1)} %shard_map.94), channel_id=1, source_target_pairs={{0,16},{8,24},{16,32},{32,48},{40,56},{48,64},{64,80},{72,88},{80,... | collective-permute-start | bytes 1572872 | tf_op jit(solution)/shard_map/ppermute | solution.py:335
  10.6 32.4 %collective-permute-start.4 = (bf16[256,1024]{1,0:T(8,128)(2,1)}, bf16[256,1024]{1,0:T(8,128)(2,1)S(1)}, u32[]{:S(2)}, u32[]{:S(2)}) collective-permute-start(bf16[256,1024]{1,0:T(8,128)(2,1)} %shard_map.94), channel_id=1, source_target_pairs={{0,8},{8,16},{16,24},{24,32},{32,40},{40,48},{48,56},{56,64},{64,7... | collective-permute-start | bytes 1572872 | tf_op jit(solution)/shard_map/ppermute | solution.py:335
  16.0 47.2 %collective-permute-start.3 = (bf16[256,1024]{1,0:T(8,128)(2,1)}, bf16[256,1024]{1,0:T(8,128)(2,1)S(1)}, u32[]{:S(2)}, u32[]{:S(2)}) collective-permute-start(bf16[256,1024]{1,0:T(8,128)(2,1)} %shard_map.93), channel_id=1, source_target_pairs={{0,32},{32,64},{64,96},{1,33},{33,65},{65,97},{2,34},{34,66},{66,9... | collective-permute-start | bytes 1572872 | tf_op jit(solution)/shard_map/ppermute | solution.py:335
  20.5 22.5 %copy-start.11 = (bf16[256,1024]{1,0:T(8,128)(2,1)}, bf16[256,1024]{1,0:T(8,128)(2,1)S(1)}, u32[]{:S(2)}) copy-start(bf16[256,1024]{1,0:T(8,128)(2,1)S(1)} %collective-permute-done.7.rest_3_) | copy-start | bytes 1572868
  20.5 44.1 %collective-permute-start.2 = (bf16[256,1024]{1,0:T(8,128)(2,1)}, bf16[256,1024]{1,0:T(8,128)(2,1)S(1)}, u32[]{:S(2)}, u32[]{:S(2)}) collective-permute-start(bf16[256,1024]{1,0:T(8,128)(2,1)} %shard_map.93), channel_id=1, source_target_pairs={{0,24},{8,32},{32,56},{40,64},{64,88},{72,96},{96,120},{1,25},{9,3... | collective-permute-start | bytes 1572872 | tf_op jit(solution)/shard_map/ppermute | solution.py:335
  33.1 9.9 %copy-start.12 = (bf16[256,1024]{1,0:T(8,128)(2,1)}, bf16[256,1024]{1,0:T(8,128)(2,1)S(1)}, u32[]{:S(2)}) copy-start(bf16[256,1024]{1,0:T(8,128)(2,1)S(1)} %collective-permute-done.6.rest_2_) | copy-start | bytes 1572868
  33.1 33.0 %collective-permute-start.1 = (bf16[256,1024]{1,0:T(8,128)(2,1)}, bf16[256,1024]{1,0:T(8,128)(2,1)}, u32[]{:S(2)}, u32[]{:S(2)}) collective-permute-start(bf16[256,1024]{1,0:T(8,128)(2,1)} %shard_map.93), channel_id=1, source_target_pairs={{0,16},{8,24},{16,32},{32,48},{40,56},{48,64},{64,80},{72,88},{80,... | collective-permute-start | bytes 1572872 | tf_op jit(solution)/shard_map/ppermute | solution.py:335
  35.2 7.8 %copy-start.13 = (bf16[256,1024]{1,0:T(8,128)(2,1)}, bf16[256,1024]{1,0:T(8,128)(2,1)S(1)}, u32[]{:S(2)}) copy-start(bf16[256,1024]{1,0:T(8,128)(2,1)S(1)} %collective-permute-done.5.rest_1_) | copy-start | bytes 1572868
  35.2 30.9 %collective-permute-start = (bf16[256,1024]{1,0:T(8,128)(2,1)}, bf16[256,1024]{1,0:T(8,128)(2,1)}, u32[]{:S(2)}, u32[]{:S(2)}) collective-permute-start(bf16[256,1024]{1,0:T(8,128)(2,1)} %shard_map.93), channel_id=1, source_target_pairs={{0,8},{8,16},{16,24},{24,32},{32,40},{40,48},{48,56},{56,64},{64,7... | collective-permute-start | bytes 1572872 | tf_op jit(solution)/shard_map/ppermute | solution.py:335
  42.9 0.8 copy-start.14
  61.9 25.3 %collective-permute-start.16 = (bf16[256,1024]{1,0:T(8,128)(2,1)}, bf16[256,1024]{1,0:T(8,128)(2,1)S(1)}, u32[]{:S(2)}, u32[]{:S(2)}) collective-permute-start(bf16[256,1024]{1,0:T(8,128)(2,1)} %get-tuple-element.40), channel_id=1, source_target_pairs={{8,0},{16,8},{24,16},{32,56},{40,32},{48,40},{56,48},{64,88},{72,6... | collective-permute-start | bytes 1572872 | tf_op jit(solution)/shard_map/ppermute | solution.py:347
  63.2 2.8 %copy-start.10 = (bf16[256,1024]{1,0:T(8,128)(2,1)}, bf16[256,1024]{1,0:T(8,128)(2,1)S(1)}, u32[]{:S(2)}) copy-start(bf16[256,1024]{1,0:T(8,128)(2,1)S(1)} %collective-permute-done.3.rest_3_) | copy-start | bytes 1572868
  63.2 25.3 %collective-permute-start.17 = (bf16[256,1024]{1,0:T(8,128)(2,1)}, bf16[256,1024]{1,0:T(8,128)(2,1)S(1)}, u32[]{:S(2)}, u32[]{:S(2)}) collective-permute-start(bf16[256,1024]{1,0:T(8,128)(2,1)} %get-tuple-element.41), channel_id=1, source_target_pairs={{16,0},{24,8},{32,48},{48,32},{56,40},{64,80},{80,64},{88,72},{96,... | collective-permute-start | bytes 1572872 | tf_op jit(solution)/shard_map/ppermute | solution.py:347
  64.6 1.5 %copy-start.15 = (bf16[256,1024]{1,0:T(8,128)(2,1)}, bf16[256,1024]{1,0:T(8,128)(2,1)S(1)}, u32[]{:S(2)}) copy-start(bf16[256,1024]{1,0:T(8,128)(2,1)S(1)} %collective-permute-done.2.rest_2_) | copy-start | bytes 1572868
  64.6 24.6 %collective-permute-start.18 = (bf16[256,1024]{1,0:T(8,128)(2,1)}, bf16[256,1024]{1,0:T(8,128)(2,1)S(1)}, u32[]{:S(2)}, u32[]{:S(2)}) collective-permute-start(bf16[256,1024]{1,0:T(8,128)(2,1)} %get-tuple-element.42), channel_id=1, source_target_pairs={{24,0},{32,40},{56,32},{64,72},{88,64},{96,104},{120,96},{25,1},{3... | collective-permute-start | bytes 1572872 | tf_op jit(solution)/shard_map/ppermute | solution.py:347
  66.1 23.1 %copy-start.9 = (bf16[256,1024]{1,0:T(8,128)(2,1)S(1)}, bf16[256,1024]{1,0:T(8,128)(2,1)}, u32[]{:S(2)}) copy-start(bf16[256,1024]{1,0:T(8,128)(2,1)} %get-tuple-element.43) | copy-start | bytes 1572868
  84.4 6.2 %copy-start.16 = (f32[1,128]{1,0:T(1,128)S(1)}, f32[1,128]{1,0:T(1,128)}, u32[]{:S(2)}) copy-start(f32[1,128]{1,0:T(1,128)} %get-tuple-element.36) | copy-start | bytes 1540
  84.4 6.2 %copy-start.17 = (f32[1,128]{1,0:T(1,128)S(1)}, f32[1,128]{1,0:T(1,128)}, u32[]{:S(2)}) copy-start(f32[1,128]{1,0:T(1,128)} %get-tuple-element.37) | copy-start | bytes 1540
  84.4 37.6 %copy-start.7 = (bf16[256,1024]{1,0:T(8,128)(2,1)S(1)}, bf16[256,1024]{1,0:T(8,128)(2,1)}, u32[]{:S(2)}) copy-start(bf16[256,1024]{1,0:T(8,128)(2,1)} %get-tuple-element.35) | copy-start | bytes 1572868
  84.5 37.6 %collective-permute-start.8 = (bf16[256,1024]{1,0:T(8,128)(2,1)}, bf16[256,1024]{1,0:T(8,128)(2,1)S(1)}, u32[]{:S(2)}, u32[]{:S(2)}) collective-permute-start(bf16[256,1024]{1,0:T(8,128)(2,1)} %get-tuple-element.32), channel_id=1, source_target_pairs={{8,0},{16,8},{24,16},{32,56},{40,32},{48,40},{56,48},{64,88},{72,6... | collective-permute-start | bytes 1572872 | tf_op jit(solution)/shard_map/ppermute | solution.py:347
  85.9 36.2 %collective-permute-start.9 = (bf16[256,1024]{1,0:T(8,128)(2,1)}, bf16[256,1024]{1,0:T(8,128)(2,1)S(1)}, u32[]{:S(2)}, u32[]{:S(2)}) collective-permute-start(bf16[256,1024]{1,0:T(8,128)(2,1)} %get-tuple-element.33), channel_id=1, source_target_pairs={{16,0},{24,8},{32,48},{48,32},{56,40},{64,80},{80,64},{88,72},{96,... | collective-permute-start | bytes 1572872 | tf_op jit(solution)/shard_map/ppermute | solution.py:347
  87.2 36.0 %copy-start.3 = (bf16[256,1024]{1,0:T(8,128)(2,1)}, bf16[256,1024]{1,0:T(8,128)(2,1)S(1)}, u32[]{:S(2)}) copy-start(bf16[256,1024]{1,0:T(8,128)(2,1)S(1)} %collective-permute-done.16.rest_0_) | copy-start | bytes 1572868
  87.2 34.9 %collective-permute-start.10 = (bf16[256,1024]{1,0:T(8,128)(2,1)}, bf16[256,1024]{1,0:T(8,128)(2,1)S(1)}, u32[]{:S(2)}, u32[]{:S(2)}) collective-permute-start(bf16[256,1024]{1,0:T(8,128)(2,1)} %get-tuple-element.34), channel_id=1, source_target_pairs={{24,0},{32,40},{56,32},{64,72},{88,64},{96,104},{120,96},{25,1},{3... | collective-permute-start | bytes 1572872 | tf_op jit(solution)/shard_map/ppermute | solution.py:347
  88.5 34.7 %copy-start.4 = (bf16[256,1024]{1,0:T(8,128)(2,1)}, bf16[256,1024]{1,0:T(8,128)(2,1)S(1)}, u32[]{:S(2)}) copy-start(bf16[256,1024]{1,0:T(8,128)(2,1)S(1)} %collective-permute-done.17.rest_1_) | copy-start | bytes 1572868
  89.2 34.0 %copy-start.5 = (bf16[256,1024]{1,0:T(8,128)(2,1)}, bf16[256,1024]{1,0:T(8,128)(2,1)S(1)}, u32[]{:S(2)}) copy-start(bf16[256,1024]{1,0:T(8,128)(2,1)S(1)} %collective-permute-done.18.rest_2_) | copy-start | bytes 1572868
  89.3 33.9 %collective-permute-start.19 = (bf16[256,1024]{1,0:T(8,128)(2,1)S(1)}, bf16[256,1024]{1,0:T(8,128)(2,1)S(1)}, u32[]{:S(2)}, u32[]{:S(2)}) collective-permute-start(bf16[256,1024]{1,0:T(8,128)(2,1)S(1)} %select_select_fusion), channel_id=1, source_target_pairs={{32,0},{40,8},{48,16},{56,24},{64,32},{72,40},{80,48},{88,56},{96,... | collective-permute-start | bytes 1572872 | tf_op jit(solution)/shard_map/ppermute | solution.py:359
  90.6 1.2 collective-permute-start.11
  91.8 3.5 %collective-permute-start.12 = (f32[1,128]{1,0:T(1,128)S(1)}, f32[1,128]{1,0:T(1,128)S(1)}, u32[]{:S(2)}, u32[]{:S(2)}) collective-permute-start(f32[1,128]{1,0:T(1,128)S(1)} %add.30), channel_id=1, source_target_pairs={{0,2},{1,3},{2,0},{3,1},{4,6},{5,7},{6,4},{7,5},{8,10},{9,11},{10,... | collective-permute-start | bytes 1544 | tf_op jit(solution)/shard_map/ppermute | solution.py:320
  95.4 5.0 %collective-permute-start.13 = (f32[1,128]{1,0:T(1,128)S(1)}, f32[1,128]{1,0:T(1,128)S(1)}, u32[]{:S(2)}, u32[]{:S(2)}) collective-permute-start(f32[1,128]{1,0:T(1,128)S(1)} %add.31), channel_id=1, source_target_pairs={{0,4},{1,5},{2,6},{3,7},{4,0},{5,1},{6,2},{7,3},{8,12},{9,13},{10,... | collective-permute-start | bytes 1544 | tf_op jit(solution)/shard_map/ppermute | solution.py:320
  100.4 16.0 %collective-permute-start.14 = (f32[1,128]{1,0:T(1,128)S(1)}, f32[1,128]{1,0:T(1,128)S(1)}, u32[]{:S(2)}, u32[]{:S(2)}) collective-permute-start(f32[1,128]{1,0:T(1,128)S(1)} %add.32), channel_id=1, source_target_pairs={{0,32},{8,40},{16,48},{24,56},{32,0},{40,8},{48,16},{56,24},{64,96... | collective-permute-start | bytes 1544 | tf_op jit(solution)/shard_map/ppermute | solution.py:320
  116.4 5.6 %collective-permute-start.15 = (f32[1,128]{1,0:T(1,128)S(1)}, f32[1,128]{1,0:T(1,128)S(1)}, u32[]{:S(2)}, u32[]{:S(2)}) collective-permute-start(f32[1,128]{1,0:T(1,128)S(1)} %add.33), channel_id=1, source_target_pairs={{0,64},{8,72},{16,80},{24,88},{32,96},{40,104},{48,112},{56,120},{... | collective-permute-start | bytes 1544 | tf_op jit(solution)/shard_map/ppermute | solution.py:320
  122.0 4.9 %copy-start = (bf16[256,1024]{1,0:T(8,128)(2,1)}, bf16[256,1024]{1,0:T(8,128)(2,1)S(1)}, u32[]{:S(2)}) copy-start(bf16[256,1024]{1,0:T(8,128)(2,1)S(1)} %collective-permute-done.8.rest_0_) | copy-start | bytes 1572868
  122.1 4.9 %copy-start.1 = (bf16[256,1024]{1,0:T(8,128)(2,1)}, bf16[256,1024]{1,0:T(8,128)(2,1)S(1)}, u32[]{:S(2)}) copy-start(bf16[256,1024]{1,0:T(8,128)(2,1)S(1)} %collective-permute-done.9.rest_1_) | copy-start | bytes 1572868
  122.1 4.9 %copy-start.2 = (bf16[256,1024]{1,0:T(8,128)(2,1)}, bf16[256,1024]{1,0:T(8,128)(2,1)S(1)}, u32[]{:S(2)}) copy-start(bf16[256,1024]{1,0:T(8,128)(2,1)S(1)} %collective-permute-done.10.rest_2_) | copy-start | bytes 1572868
  123.2 0.8 copy-start.8
  127.0 18.7 %collective-permute-start.20 = (bf16[256,1024]{1,0:T(8,128)(2,1)}, bf16[256,1024]{1,0:T(8,128)(2,1)S(1)}, u32[]{:S(2)}, u32[]{:S(2)}) collective-permute-start(bf16[256,1024]{1,0:T(8,128)(2,1)} %select_select_fusion.1), channel_id=1, source_target_pairs={{32,0},{40,8},{48,16},{56,24},{64,32},{72,40},{80,48},{88,56},{96,... | collective-permute-start | bytes 1572872 | tf_op jit(solution)/shard_map/ppermute | solution.py:359
  128.3 3.6 %collective-permute-start.21 = (f32[1,128]{1,0:T(1,128)S(1)}, f32[1,128]{1,0:T(1,128)S(1)}, u32[]{:S(2)}, u32[]{:S(2)}) collective-permute-start(f32[1,128]{1,0:T(1,128)S(1)} %add.34), channel_id=1, source_target_pairs={{0,8},{8,0},{16,24},{24,16},{32,40},{40,32},{48,56},{56,48},{64,72... | collective-permute-start | bytes 1544 | tf_op jit(solution)/shard_map/ppermute | solution.py:320
  131.9 5.0 %collective-permute-start.22 = (f32[1,128]{1,0:T(1,128)S(1)}, f32[1,128]{1,0:T(1,128)S(1)}, u32[]{:S(2)}, u32[]{:S(2)}) collective-permute-start(f32[1,128]{1,0:T(1,128)S(1)} %add.35), channel_id=1, source_target_pairs={{0,16},{8,24},{16,0},{24,8},{32,48},{40,56},{48,32},{56,40},{64,80... | collective-permute-start | bytes 1544 | tf_op jit(solution)/shard_map/ppermute | solution.py:320
  145.6 0.8 copy-start.6
